TPU v7x, 128 devices: a whole 4x4x4 slice. The times are simulated.
128 devices in a mesh: dp: 8 (over y, core), sp: 2 (over z_hi), tp: 8 (over x, z_lo).
Axes of the slice: x: 4, y: 4, z: 4 (z_hi: 2, z_lo: 2; z = z_hi * 2 + z_lo), core: 2. Of those that a mesh axis runs over, the one named last changes fastest.
Arguments:
- tokens: bfloat16 [16384, 2048], P(('dp', 'sp')), may hold values from -6 to 6
- cotangent: bfloat16 [16384, 2048], P(('dp', 'sp')), may hold values from -6 to 6
- seq_lens: int32 [8, 2], P('dp'), may hold values from 0 to 2048, as said below
- owners: int32 [4, 16], replicated, may hold values from 0 to 15, each once within a row
- shared_vec: float32 [6, 2048], replicated, may hold values from -1.5 to 1.6
- shared_first: float32 [6, 2048], replicated, may hold values from -768 to 768
- shared_second: float32 [6, 2048], replicated, may hold values from 16384 to 65536
- split_vec: float32 [8, 1792], P('tp'), may hold values from -0.75 to 0.75
- split_first: float32 [8, 1792], P('tp'), may hold values from -384 to 384
- split_second: float32 [8, 1792], P('tp'), may hold values from 4096 to 16384
- qkv_master: float32 [16, 128, 6144], P(('dp', 'sp'), None, 'tp'), may hold values from -0.125 to 0.125
- qkv_first: float32 [16, 128, 6144], P(('dp', 'sp'), None, 'tp'), may hold values from -1536 to 1536
- qkv_second: float32 [16, 128, 6144], P(('dp', 'sp'), None, 'tp'), may hold values from 65536 to 262144
- qkv_left: float32 [16, 8, 128, 128], P(('dp', 'sp'), 'tp'), may hold values from -1 to 1, as said below
- qkv_right: float32 [16, 8, 768, 768], P(('dp', 'sp'), 'tp'), may hold values from -1 to 1, as said below
- out_master: float32 [2048, 16, 128], P('tp', ('dp', 'sp')), may hold values from -1.5 to 1.5
- out_first: float32 [2048, 16, 128], P('tp', ('dp', 'sp')), may hold values from -80 to 80
- out_second: float32 [2048, 16, 128], P('tp', ('dp', 'sp')), may hold values from 163.84 to 655.36
- out_left: float32 [16, 8, 256, 256], P(('dp', 'sp'), 'tp'), may hold values from -1 to 1, as said below
- out_right: float32 [16, 8, 128, 128], P(('dp', 'sp'), 'tp'), may hold values from -1 to 1, as said below
- up_master: float32 [16, 128, 8192], P(('dp', 'sp'), None, 'tp'), may hold values from -0.125 to 0.125
- up_first: float32 [16, 128, 8192], P(('dp', 'sp'), None, 'tp'), may hold values from -224 to 224
- up_second: float32 [16, 128, 8192], P(('dp', 'sp'), None, 'tp'), may hold values from 1474.56 to 5898.24
- up_left: float32 [16, 8, 128, 128], P(('dp', 'sp'), 'tp'), may hold values from -1 to 1, as said below
- up_right: float32 [16, 8, 1024, 1024], P(('dp', 'sp'), 'tp'), may hold values from -1 to 1, as said below
- down_master: float32 [8192, 16, 128], P('tp', ('dp', 'sp')), may hold values from -0.0625 to 0.0625
- down_first: float32 [8192, 16, 128], P('tp', ('dp', 'sp')), may hold values from -448 to 448
- down_second: float32 [8192, 16, 128], P('tp', ('dp', 'sp')), may hold values from 5898.24 to 23592.96
- down_left: float32 [16, 8, 1024, 1024], P(('dp', 'sp'), 'tp'), may hold values from -1 to 1, as said below
- down_right: float32 [16, 8, 128, 128], P(('dp', 'sp'), 'tp'), may hold values from -1 to 1, as said below
Outputs:
- output: bfloat16 [16384, 2048], P(('dp', 'sp'))
- grad_input: bfloat16 [16384, 2048], P(('dp', 'sp'))
- shared_new: float32 [6, 2048], replicated
- shared_first_new: float32 [6, 2048], replicated
- shared_second_new: float32 [6, 2048], replicated
- split_new: float32 [8, 1792], P('tp')
- split_first_new: float32 [8, 1792], P('tp')
- split_second_new: float32 [8, 1792], P('tp')
- qkv_new: float32 [16, 128, 6144], P(('dp', 'sp'), None, 'tp')
- qkv_first_new: float32 [16, 128, 6144], P(('dp', 'sp'), None, 'tp')
- qkv_second_new: float32 [16, 128, 6144], P(('dp', 'sp'), None, 'tp')
- qkv_copy: bfloat16 [16, 128, 6144], P(('dp', 'sp'), None, 'tp')
- out_new: float32 [2048, 16, 128], P('tp', ('dp', 'sp'))
- out_first_new: float32 [2048, 16, 128], P('tp', ('dp', 'sp'))
- out_second_new: float32 [2048, 16, 128], P('tp', ('dp', 'sp'))
- out_copy: bfloat16 [2048, 16, 128], P('tp', ('dp', 'sp'))
- up_new: float32 [16, 128, 8192], P(('dp', 'sp'), None, 'tp')
- up_first_new: float32 [16, 128, 8192], P(('dp', 'sp'), None, 'tp')
- up_second_new: float32 [16, 128, 8192], P(('dp', 'sp'), None, 'tp')
- up_copy: bfloat16 [16, 128, 8192], P(('dp', 'sp'), None, 'tp')
- down_new: float32 [8192, 16, 128], P('tp', ('dp', 'sp'))
- down_first_new: float32 [8192, 16, 128], P('tp', ('dp', 'sp'))
- down_second_new: float32 [8192, 16, 128], P('tp', ('dp', 'sp'))
- down_copy: bfloat16 [8192, 16, 128], P('tp', ('dp', 'sp'))
Inputs may be any that keep to these rules, and one draw needn't show every extreme that they name: `seq_lens`: each group holds either one sequence of 2048 tokens (second entry 0) or two of 1024; every draw has groups of both kinds. `owners`: each row is a permutation of the slots. `qkv_left`: each square matrix is orthogonal. `qkv_right`: each square matrix is orthogonal. `out_left`: each square matrix is orthogonal. `out_right`: each square matrix is orthogonal. `up_left`: each square matrix is orthogonal. `up_right`: each square matrix is orthogonal. `down_left`: each square matrix is orthogonal. `down_right`: each square matrix is orthogonal.
All inputs are finite; a program needn't handle non-finite values.
Results may differ from a plain program's by a relative error of at most 0.0065.
The roundings to bfloat16 on the way count: a program that leaves them out, or rounds other values in their place, can miss the bound.
Values may be sent and summed in bfloat16 or wider, within the bound.
No kernel may reach another device: no remote copies, remote signals or barrier semaphores. Data moves between devices by JAX's collectives and lax.ppermute only.
A program may use at most 256 MiB of HBM per device.

v0:
```python
import jax
import jax.numpy as jnp
from jax import lax
from jax.sharding import PartitionSpec as P

D = 2048
H = 8
STEP = 5


ln_eps = 1e-05
adam_eps = 1e-08
beta_one = 0.5
beta_two = 0.5
rate_qkv = 0.01
rate_out = 0.05
rate_up = 0.01
rate_down = 0.005
rate_vector = 0.2
weight_decay = 0.01


def exact_dot(left_matrix, right_matrix):
    return jnp.dot(
        left_matrix,
        right_matrix,
        precision=lax.Precision.HIGHEST,
        preferred_element_type=jnp.float32,
    )


def contract_rows(left_matrix, right_matrix):
    return lax.dot_general(
        left_matrix, right_matrix, (((0,), (0,)), ((), ())), preferred_element_type=jnp.float32
    )


def contract_cols(left_matrix, right_matrix):
    return lax.dot_general(
        left_matrix, right_matrix, (((1,), (1,)), ((), ())), preferred_element_type=jnp.float32
    )


def layer_norm(field, gain, shift):
    center = field - jnp.mean(field, axis=-1, keepdims=True)
    spread = jnp.mean(center * center, axis=-1, keepdims=True)
    return center * lax.rsqrt(spread + ln_eps) * gain + shift


def gelu_exact(field):
    return jax.nn.gelu(field, approximate=False)


def rotate(field, places, rot_dims):
    half_dims = rot_dims // 2
    frequency = 10000.0 ** (-2.0 * jnp.arange(half_dims, dtype=jnp.float32) / rot_dims)
    angles = places.astype(jnp.float32)[:, None] * frequency[None, :]
    cosine = jnp.cos(angles)[:, None, :]
    sine_part = jnp.sin(angles)[:, None, :]
    front = field[..., :half_dims]
    middle = field[..., half_dims:rot_dims]
    return jnp.concatenate(
        [
            front * cosine - middle * sine_part,
            middle * cosine + front * sine_part,
            field[..., rot_dims:],
        ],
        axis=-1,
    )


def row_places(first_len, second_len, part_index, local_index, part_count):
    first_rows = first_len // part_count
    in_first = local_index < first_rows
    segment = jnp.where(in_first, 0, 1).astype(jnp.int32)
    position = jnp.where(
        in_first,
        part_index * first_rows + local_index,
        part_index * (second_len // part_count) + local_index - first_rows,
    )
    return (segment, position)


def soap_block(gradient, weight, first_moment, second_moment, left_basis, right_basis, step_rate):
    turned = exact_dot(exact_dot(left_basis.T, gradient), right_basis)
    first_new = beta_one * first_moment + (1.0 - beta_one) * turned
    second_new = beta_two * second_moment + (1.0 - beta_two) * turned * turned
    direction = (
        first_new
        / (1.0 - beta_one**STEP)
        / (jnp.sqrt(second_new / (1.0 - beta_two**STEP)) + adam_eps)
    )
    returned = exact_dot(exact_dot(left_basis, direction), right_basis.T)
    return (weight * (1.0 - step_rate * weight_decay) - step_rate * returned, first_new, second_new)


def adam_vector(gradient, current, first_moment, second_moment):
    first_new = beta_one * first_moment + (1.0 - beta_one) * gradient
    second_new = beta_two * second_moment + (1.0 - beta_two) * gradient * gradient
    direction = (
        first_new
        / (1.0 - beta_one**STEP)
        / (jnp.sqrt(second_new / (1.0 - beta_two**STEP)) + adam_eps)
    )
    return (current - rate_vector * direction, first_new, second_new)


def inverse_of(order):
    amount = order.shape[0]
    slot_index = jnp.arange(amount, dtype=jnp.int32)
    matches = order[None, :] == slot_index[:, None]
    return jnp.sum(jnp.where(matches, slot_index[None, :], 0), axis=1)


def unslot_all(gathered, owners):
    qkv_slots, out_slots, up_slots, down_slots = gathered
    w_qkv = jnp.take(qkv_slots, owners[0], axis=0).reshape(-1, qkv_slots.shape[2])
    w_out = jnp.take(out_slots, owners[1], axis=1).reshape(out_slots.shape[0], -1)
    w_up = jnp.take(up_slots, owners[2], axis=0).reshape(-1, up_slots.shape[2])
    w_down = jnp.take(down_slots, owners[3], axis=1).reshape(down_slots.shape[0], -1)
    return (w_qkv, w_out, w_up, w_down)


def per_device(
    tokens,
    cotangent,
    seq_lens,
    owners,
    shared_vec,
    shared_first,
    shared_second,
    split_vec,
    split_first,
    split_second,
    qkv_master,
    qkv_first,
    qkv_second,
    qkv_left,
    qkv_right,
    out_master,
    out_first,
    out_second,
    out_left,
    out_right,
    up_master,
    up_first,
    up_second,
    up_left,
    up_right,
    down_master,
    down_first,
    down_second,
    down_left,
    down_right,
):
    row_count = tokens.shape[0]
    head_size = D // H
    qkv_cols = qkv_master.shape[2]
    heads_dev = qkv_cols // (3 * head_size)
    sp_count = lax.axis_size("sp")
    sp_rank = lax.axis_index("sp")
    tp_count = lax.axis_size("tp")
    tp_rank = lax.axis_index("tp")
    share_rows = row_count // tp_count
    scale = head_size ** (-0.5)
    rot_dims = head_size // 4
    qkv_low = qkv_master.astype(jnp.bfloat16)
    out_low = out_master.astype(jnp.bfloat16)
    up_low = up_master.astype(jnp.bfloat16)
    down_low = down_master.astype(jnp.bfloat16)
    fetched = (
        lax.all_gather(qkv_low, ("dp", "sp"), axis=0, tiled=True),
        lax.all_gather(out_low, ("dp", "sp"), axis=1, tiled=True),
        lax.all_gather(up_low, ("dp", "sp"), axis=0, tiled=True),
        lax.all_gather(down_low, ("dp", "sp"), axis=1, tiled=True),
    )
    w_qkv, w_out, w_up, w_down = unslot_all(fetched, owners)
    field = tokens.astype(jnp.float32)
    h_one = layer_norm(field, shared_vec[0], shared_vec[1]).astype(jnp.bfloat16)
    h_two = layer_norm(field, shared_vec[2], shared_vec[3]).astype(jnp.bfloat16)
    b_qkv = split_vec[0, :qkv_cols]
    b_up = split_vec[0, qkv_cols:]
    qkv_raw = (jnp.dot(h_one, w_qkv, preferred_element_type=jnp.float32) + b_qkv).reshape(
        row_count, heads_dev, 3, head_size
    )
    local_index = jnp.arange(row_count, dtype=jnp.int32)
    query_seg, query_pos = row_places(
        seq_lens[0, 0], seq_lens[0, 1], sp_rank, local_index, sp_count
    )

    def turned(values_in):
        return rotate(values_in, query_pos, rot_dims)

    query_raw = qkv_raw[:, :, 0]
    key_raw = qkv_raw[:, :, 1]
    query_low = turned(query_raw).astype(jnp.bfloat16)
    key_low = turned(key_raw).astype(jnp.bfloat16)
    value_low = qkv_raw[:, :, 2].astype(jnp.bfloat16)
    key_all, value_all = (
        lax.all_gather(key_low, "sp", axis=0, tiled=True),
        lax.all_gather(value_low, "sp", axis=0, tiled=True),
    )
    key_index = jnp.arange(sp_count * row_count, dtype=jnp.int32)
    key_seg, key_pos = row_places(
        seq_lens[0, 0], seq_lens[0, 1], key_index // row_count, key_index % row_count, sp_count
    )
    block_rows = min(512, row_count)
    block_count = row_count // block_rows

    def scores_of(query_block, seg_part, pos_part, keys_in):
        visible = (seg_part[:, None] == key_seg[None, :]) & (key_pos[None, :] <= pos_part[:, None])
        raw_scores = (
            jnp.einsum("qhd,khd->hqk", query_block, keys_in, preferred_element_type=jnp.float32)
            * scale
        )
        return jnp.where(visible[None], raw_scores, -1e30)

    def forward_block(items):
        query_block, seg_part, pos_part = items
        scores = scores_of(query_block, seg_part, pos_part, key_all)
        maximum = jnp.max(scores, axis=-1, keepdims=True)
        exponent = jnp.exp(scores - maximum)
        denominator = jnp.sum(exponent, axis=-1, keepdims=True)
        weights_low = (exponent / denominator).astype(jnp.bfloat16)
        attended_block = jnp.einsum(
            "hqk,khd->qhd", weights_low, value_all, preferred_element_type=jnp.float32
        )
        return (attended_block, maximum[..., 0] + jnp.log(denominator[..., 0]))

    query_blocks = query_low.reshape(block_count, block_rows, heads_dev, head_size)
    seg_blocks = query_seg.reshape(block_count, block_rows)
    pos_blocks = query_pos.reshape(block_count, block_rows)
    attended, log_sums = lax.map(forward_block, (query_blocks, seg_blocks, pos_blocks))
    attended_low = attended.reshape(row_count, heads_dev * head_size).astype(jnp.bfloat16)
    pre_act = jnp.dot(h_two, w_up, preferred_element_type=jnp.float32) + b_up
    hidden_low = gelu_exact(pre_act).astype(jnp.bfloat16)
    partial_out = jnp.dot(attended_low, w_out, preferred_element_type=jnp.float32) + jnp.dot(
        hidden_low, w_down, preferred_element_type=jnp.float32
    )
    branches = lax.psum(partial_out, "tp")
    output = (field + branches + shared_vec[4] + shared_vec[5]).astype(jnp.bfloat16)
    refetched = (
        lax.all_gather(qkv_low, ("dp", "sp"), axis=0, tiled=True),
        lax.all_gather(out_low, ("dp", "sp"), axis=1, tiled=True),
        lax.all_gather(up_low, ("dp", "sp"), axis=0, tiled=True),
        lax.all_gather(down_low, ("dp", "sp"), axis=1, tiled=True),
    )
    w_qkv, w_out, w_up, w_down = unslot_all(refetched, owners)
    key_all, value_all = (
        lax.all_gather(key_low, "sp", axis=0, tiled=True),
        lax.all_gather(value_low, "sp", axis=0, tiled=True),
    )
    grad_out_w = contract_rows(attended_low, cotangent)
    grad_down_w = contract_rows(hidden_low, cotangent)
    grad_attended = (
        contract_cols(cotangent, w_out)
        .astype(jnp.bfloat16)
        .reshape(row_count, heads_dev, head_size)
    )
    grad_hidden = contract_cols(cotangent, w_down)
    gelu_back = jax.vjp(gelu_exact, pre_act)[1]
    grad_pre = gelu_back(grad_hidden)[0].astype(jnp.bfloat16)
    grad_up_w = contract_rows(h_two, grad_pre)
    grad_h_two = contract_cols(grad_pre, w_up)

    def backward_block(carry, items):
        key_sum, value_sum = carry
        query_block, seg_part, pos_part, log_part, grad_block = items
        scores = scores_of(query_block, seg_part, pos_part, key_all)
        probability = jnp.exp(scores - log_part[..., None])
        grad_probs = jnp.einsum(
            "qhd,khd->hqk", grad_block, value_all, preferred_element_type=jnp.float32
        )
        inner = jnp.sum(grad_probs * probability, axis=-1, keepdims=True)
        grad_scores = (probability * (grad_probs - inner) * scale).astype(jnp.bfloat16)
        grad_query = jnp.einsum(
            "hqk,khd->qhd", grad_scores, key_all, preferred_element_type=jnp.float32
        )
        key_sum = key_sum + jnp.einsum(
            "hqk,qhd->khd", grad_scores, query_block, preferred_element_type=jnp.float32
        )
        value_sum = value_sum + jnp.einsum(
            "hqk,qhd->khd",
            probability.astype(jnp.bfloat16),
            grad_block,
            preferred_element_type=jnp.float32,
        )
        return ((key_sum, value_sum), grad_query)

    empty_sum = jnp.zeros((sp_count * row_count, heads_dev, head_size), jnp.float32)
    grad_blocks = grad_attended.reshape(block_count, block_rows, heads_dev, head_size)
    (key_sum, value_sum), grad_query = lax.scan(
        backward_block,
        (empty_sum, empty_sum),
        (query_blocks, seg_blocks, pos_blocks, log_sums, grad_blocks),
    )
    grad_key, grad_value = (
        lax.psum_scatter(key_sum, "sp", scatter_dimension=0, tiled=True),
        lax.psum_scatter(value_sum, "sp", scatter_dimension=0, tiled=True),
    )
    query_back = jax.vjp(turned, query_raw)[1]
    key_back = jax.vjp(turned, key_raw)[1]
    grad_qkv = jnp.stack(
        [
            query_back(grad_query.reshape(row_count, heads_dev, head_size))[0],
            key_back(grad_key)[0],
            grad_value,
        ],
        axis=2,
    )
    grad_qkv = grad_qkv.reshape(row_count, qkv_cols).astype(jnp.bfloat16)
    grad_qkv_w = contract_rows(h_one, grad_qkv)
    grad_h_one = contract_cols(grad_qkv, w_qkv)
    grad_y = cotangent.astype(jnp.float32)
    center = field - jnp.mean(field, axis=-1, keepdims=True)
    inverse_std = lax.rsqrt(jnp.mean(center * center, axis=-1, keepdims=True) + ln_eps)
    unit = center * inverse_std
    sum_one, sum_two = lax.psum((grad_h_one, grad_h_two), "tp")
    norm_one_back = jax.vjp(layer_norm, field, shared_vec[0], shared_vec[1])[1]
    norm_two_back = jax.vjp(layer_norm, field, shared_vec[2], shared_vec[3])[1]
    grad_x_one = norm_one_back(sum_one)[0]
    grad_x_two = norm_two_back(sum_two)[0]
    grad_input = (grad_y + grad_x_one + grad_x_two).astype(jnp.bfloat16)
    own_rows = (local_index // share_rows == tp_rank)[:, None]
    gain_one_part = jnp.sum(jnp.where(own_rows, sum_one * unit, 0.0), axis=0)
    gain_two_part = jnp.sum(jnp.where(own_rows, sum_two * unit, 0.0), axis=0)
    shift_one_part = jnp.sum(jnp.where(own_rows, sum_one, 0.0), axis=0)
    shift_two_part = jnp.sum(jnp.where(own_rows, sum_two, 0.0), axis=0)
    bias_share = jnp.sum(jnp.where(own_rows, grad_y, 0.0), axis=0)
    shared_part = jnp.stack(
        [gain_one_part, shift_one_part, gain_two_part, shift_two_part, bias_share, bias_share]
    )
    split_part = jnp.concatenate(
        [
            jnp.sum(grad_qkv.astype(jnp.float32), axis=0),
            jnp.sum(grad_pre.astype(jnp.float32), axis=0),
        ]
    )[None, :]
    shared_grad = lax.psum(shared_part, ("dp", "sp", "tp"))
    split_grad = lax.psum(split_part, ("dp", "sp"))
    group_count = owners.shape[1]
    slot_qkv = jnp.take(
        grad_qkv_w.reshape(group_count, -1, qkv_cols), inverse_of(owners[0]), axis=0
    )
    slot_out = jnp.take(
        grad_out_w.reshape(grad_out_w.shape[0], group_count, -1), inverse_of(owners[1]), axis=1
    )
    slot_up = jnp.take(
        grad_up_w.reshape(group_count, -1, grad_up_w.shape[1]), inverse_of(owners[2]), axis=0
    )
    slot_down = jnp.take(
        grad_down_w.reshape(grad_down_w.shape[0], group_count, -1), inverse_of(owners[3]), axis=1
    )
    sum_qkv, sum_out, sum_up, sum_down = (
        lax.psum_scatter(slot_qkv, ("dp", "sp"), scatter_dimension=0, tiled=True),
        lax.psum_scatter(slot_out, ("dp", "sp"), scatter_dimension=1, tiled=True),
        lax.psum_scatter(slot_up, ("dp", "sp"), scatter_dimension=0, tiled=True),
        lax.psum_scatter(slot_down, ("dp", "sp"), scatter_dimension=1, tiled=True),
    )
    new_qkv = soap_block(
        sum_qkv[0],
        qkv_master[0],
        qkv_first[0],
        qkv_second[0],
        qkv_left[0, 0],
        qkv_right[0, 0],
        rate_qkv,
    )
    new_out = soap_block(
        sum_out[:, 0],
        out_master[:, 0],
        out_first[:, 0],
        out_second[:, 0],
        out_left[0, 0],
        out_right[0, 0],
        rate_out,
    )
    new_up = soap_block(
        sum_up[0], up_master[0], up_first[0], up_second[0], up_left[0, 0], up_right[0, 0], rate_up
    )
    new_down = soap_block(
        sum_down[:, 0],
        down_master[:, 0],
        down_first[:, 0],
        down_second[:, 0],
        down_left[0, 0],
        down_right[0, 0],
        rate_down,
    )
    new_shared = adam_vector(shared_grad, shared_vec, shared_first, shared_second)
    new_split = adam_vector(split_grad, split_vec, split_first, split_second)
    return (
        output,
        grad_input,
        new_shared[0],
        new_shared[1],
        new_shared[2],
        new_split[0],
        new_split[1],
        new_split[2],
        new_qkv[0][None],
        new_qkv[1][None],
        new_qkv[2][None],
        new_qkv[0][None].astype(jnp.bfloat16),
        new_out[0][:, None],
        new_out[1][:, None],
        new_out[2][:, None],
        new_out[0][:, None].astype(jnp.bfloat16),
        new_up[0][None],
        new_up[1][None],
        new_up[2][None],
        new_up[0][None].astype(jnp.bfloat16),
        new_down[0][:, None],
        new_down[1][:, None],
        new_down[2][:, None],
        new_down[0][:, None].astype(jnp.bfloat16),
    )


def solution(mesh):
    in_specs = (
        P(("dp", "sp"), None),
        P(("dp", "sp"), None),
        P("dp", None),
        P(),
        P(),
        P(),
        P(),
        P("tp", None),
        P("tp", None),
        P("tp", None),
        P(("dp", "sp"), None, "tp"),
        P(("dp", "sp"), None, "tp"),
        P(("dp", "sp"), None, "tp"),
        P(("dp", "sp"), "tp", None, None),
        P(("dp", "sp"), "tp", None, None),
        P("tp", ("dp", "sp"), None),
        P("tp", ("dp", "sp"), None),
        P("tp", ("dp", "sp"), None),
        P(("dp", "sp"), "tp", None, None),
        P(("dp", "sp"), "tp", None, None),
        P(("dp", "sp"), None, "tp"),
        P(("dp", "sp"), None, "tp"),
        P(("dp", "sp"), None, "tp"),
        P(("dp", "sp"), "tp", None, None),
        P(("dp", "sp"), "tp", None, None),
        P("tp", ("dp", "sp"), None),
        P("tp", ("dp", "sp"), None),
        P("tp", ("dp", "sp"), None),
        P(("dp", "sp"), "tp", None, None),
        P(("dp", "sp"), "tp", None, None),
    )
    out_specs = (
        P(("dp", "sp"), None),
        P(("dp", "sp"), None),
        P(),
        P(),
        P(),
        P("tp", None),
        P("tp", None),
        P("tp", None),
        P(("dp", "sp"), None, "tp"),
        P(("dp", "sp"), None, "tp"),
        P(("dp", "sp"), None, "tp"),
        P(("dp", "sp"), None, "tp"),
        P("tp", ("dp", "sp"), None),
        P("tp", ("dp", "sp"), None),
        P("tp", ("dp", "sp"), None),
        P("tp", ("dp", "sp"), None),
        P(("dp", "sp"), None, "tp"),
        P(("dp", "sp"), None, "tp"),
        P(("dp", "sp"), None, "tp"),
        P(("dp", "sp"), None, "tp"),
        P("tp", ("dp", "sp"), None),
        P("tp", ("dp", "sp"), None),
        P("tp", ("dp", "sp"), None),
        P("tp", ("dp", "sp"), None),
    )
    return jax.shard_map(
        per_device, mesh=mesh, in_specs=in_specs, out_specs=out_specs, check_vma=False
    )
```

profile of v0, /device:TPU:0, one launch (start us, length us, event | category | flops | bytes accessed | tf_op | source)
XLA Modules:
  0.0 1740.1 jit_solution(8519103695739669757)
XLA Ops:
  11.7 3.2 convert_reduce_fusion
  17.5 48.4 %all-gather.8.cloned.1.call-done = bf16[16,128,768]{2,1,0:T(8,128)(2,1)} async-done(((bf16[1,128,768]{2,1,0:T(8,128)(2,1)}), bf16[16,128,768]{2,1,0:T(8,128)(2,1)}) %all-gather.8.cloned.1.call-update) | async-done | bytes 3145744 | tf_op jit(solution)/shard_map/all_gather | solution.py:172
  65.9 4.3 gather_fusion.4
  70.2 2.4 broadcast_select_fusion.3
  73.3 4.1 convolution_add_fusion.1
  94.4 18.3 %all-gather.12.cloned.1.call-done = bf16[256,16,128]{2,0,1:T(8,128)(2,1)} async-done(((bf16[256,1,128]{2,0,1:T(8,128)(2,1)}), bf16[256,16,128]{2,0,1:T(8,128)(2,1)}) %all-gather.12.cloned.1.call-update) | async-done | bytes 1048592 | tf_op jit(solution)/shard_map/all_gather | solution.py:173
  112.7 2.1 gather_fusion.5
  118.1 4.7 fusion.118
  129.6 9.5 all-gather.18.cloned.1.call-done
  140.5 25.3 %all-gather.10.cloned.1.call-done = bf16[2048,1,256]{0,2,1:T(8,128)(2,1)} async-done(((bf16[1024,1,256]{0,2,1:T(8,128)(2,1)}), bf16[2048,1,256]{0,2,1:T(8,128)(2,1)}) %all-gather.10.cloned.1.call-update) | async-done | bytes 1048592 | tf_op jit(solution)/shard_map/all_gather | solution.py:200
  165.9 2.3 copy.172
  168.1 10.7 while.33
  168.1 2.6 fusion.329
  173.5 2.6 fusion.329
  178.8 21.7 %while.34 = (s32[]{:T(128)}, f32[2048,1,256]{0,2,1:T(8,128)}, f32[2048,1,256]{0,2,1:T(8,128)}, f32[2,512,1,256]{3,1,2,0:T(8,128)}, bf16[2,512,1,256]{3,1,2,0:T(8...) while((s32[]{:T(128)}, f32[2048,1,256]{0,2,1:T(8,128)}, ...), condition=%wide.region_9.14_spmd.clone.clone.clone.clone, body=%wide.region_7.0_spmd.clone.clone.clone.sunk.clone | while | flops 2700123648 | bytes 94951864 | solution.py:292
  178.9 2.9 subtract_exponential_fusion.4
  189.7 2.9 subtract_exponential_fusion.4
  205.8 18.2 %all-gather.16.cloned.1.call-done = bf16[1024,16,128]{2,0,1:T(8,128)(2,1)} async-done(((bf16[1024,1,128]{2,0,1:T(8,128)(2,1)}), bf16[1024,16,128]{2,0,1:T(8,128)(2,1)}) %all-gather.16.cloned.1.call-update) | async-done | bytes 4194320 | tf_op jit(solution)/shard_map/all_gather | solution.py:175
  224.1 5.3 gather_fusion.7
  229.3 4.7 select_bitcast_fusion.1
  234.0 6.6 copy.177
  240.6 41.1 %all-gather.14.cloned.1.call-done = bf16[16,128,1024]{2,1,0:T(8,128)(2,1)} async-done(((bf16[1,128,1024]{2,1,0:T(8,128)(2,1)}), bf16[16,128,1024]{2,1,0:T(8,128)(2,1)}) %all-gather.14.cloned.1.call-update) | async-done | bytes 4194320 | tf_op jit(solution)/shard_map/all_gather | solution.py:174
  281.7 5.0 gather_fusion.6
  286.7 2.8 broadcast_select_fusion.1
  290.2 15.2 multiply_convert_fusion.1
  305.4 4.6 fusion.257
  310.0 4.6 convolution_add_fusion
  314.6 8.4 convert_reduce_fusion.1
  324.3 6.9 fusion.259
  335.8 20.6 %reduce-scatter.9.cloned.1.call-done = f32[1024,1,256]{0,2,1:T(8,128)} async-done(((f32[2048,1,256]{0,2,1:T(8,128)}), f32[1024,1,256]{0,2,1:T(8,128)}) %reduce-scatter.9.cloned.1.call-update) | async-done | bytes 1048592 | tf_op jit(solution)/shard_map/reduce_scatter | solution.py:299
  360.6 5.6 fusion.258
  366.3 6.5 copy.209
  373.0 5.7 fusion.261
  378.7 3.6 gather_fusion.1
  382.3 3.2 select_bitcast_fusion.2
  386.1 11.1 fusion.242
  397.2 7.8 gather_fusion.2
  405.0 8.7 broadcast_select_fusion
  413.9 7.1 convolution_bitcast_fusion.3
  421.0 4.1 copy.215
  425.1 7.8 gather_fusion.3
  432.9 7.6 select_bitcast_fusion
  440.9 896.8 %all-reduce.9.cloned.1.call-done = (f32[1024,2048]{1,0:T(8,128)}, f32[1024,2048]{1,0:T(8,128)}, f32[1024,2048]{1,0:T(8,128)}) async-done(((f32[1024,2048]{1,0:T(8,128)}, f32[1024,2048]{1,0:T(8,128)}, f32[1024,2048]{1,0:T(8,128)}), (f32[1024,2048]{1,0:T(8,128)}, f32[1024,2048]{1,0:T(8,128)}, f32[1024,2048]{1,0:T(8,128)})) %all-reduce.9.cloned.1.call-update) | async-done | bytes 25165840 | tf_op jit(solution)/shard_map/psum | solution.py:240
  1337.7 9.5 fusion.85
  1347.2 2.3 slice-done
  1350.9 14.4 fusion.81
  1365.3 15.2 fusion.246
  1380.5 6.5 copy.206
  1387.0 8.8 fusion.260
  1395.8 6.5 gather_fusion
  1402.3 6.2 broadcast_select_fusion.2
  1408.5 11.1 reduce-scatter.13.cloned.1.call-done
  1425.5 36.5 %psum.39 = f32[1,1792]{1,0:T(1,128)S(1)} all-reduce(f32[1,1792]{1,0:T(1,128)S(1)} %broadcast_in_dim.288), channel_id=1, replica_groups=mesh['dp'=8,'sp'=2,'tp'=8] {'dp','sp'}, use_global_device_ids=true, to_apply=%region_26.31 | all-reduce | flops 1792 | bytes 14336 | tf_op jit(solution)/shard_map/psum | solution.py:340
  1463.4 62.2 %reduce-scatter.15.cloned.1.call-done = f32[1,128,1024]{2,1,0:T(8,128)} async-done(((f32[16,128,1024]{2,1,0:T(8,128)}), f32[1,128,1024]{2,1,0:T(8,128)}) %reduce-scatter.15.cloned.1.call-update) | async-done | bytes 524304 | tf_op jit(solution)/shard_map/reduce_scatter | solution.py:357
  1527.6 4.8 fusion.97
  1532.5 2.3 fusion.142
  1534.8 4.6 fusion.119
  1541.0 90.1 %reduce-scatter.17.cloned.1.call-done = f32[1024,1,128]{2,0,1:T(8,128)} async-done(((f32[1024,16,128]{2,0,1:T(8,128)}), f32[1024,1,128]{2,0,1:T(8,128)}) %reduce-scatter.17.cloned.1.call-update) | async-done | bytes 524304 | tf_op jit(solution)/shard_map/reduce_scatter | solution.py:358
  1631.0 4.9 fusion.93
  1637.1 4.8 fusion.91
  1645.7 71.9 %psum.38 = f32[6,2048]{1,0:T(8,128)S(1)} all-reduce(f32[6,2048]{1,0:T(8,128)S(1)} %stack.40), channel_id=1, replica_groups=mesh['dp'=8,'sp'=2,'tp'=8] {'dp','sp','tp'}, use_global_device_ids=true, to_apply=%region_23.28 | all-reduce | flops 12288 | bytes 98304 | tf_op jit(solution)/shard_map/psum | solution.py:339
  1719.1 4.9 reduce-scatter.11.cloned.1.call-done
  1727.4 2.1 fusion.151
  1730.5 2.1 fusion.126
  (350 shorter events, 92.5 us)
Async XLA Ops:
  7.2 1718.7 %copy-start = (f32[1,1,768,768]{3,2,1,0:T(8,128)S(1)}, f32[1,1,768,768]{3,2,1,0:T(8,128)}, u32[]{:S(2)}) copy-start(f32[1,1,768,768]{3,2,1,0:T(8,128)} %param.56) | copy-start | bytes 7077892
  7.2 58.7 %all-gather.8.cloned.1.call-start = ((), (), s32[]{:S(2)}) async-start(), calls=%async_computation.6 | async-start | bytes 3342336 | tf_op jit(solution)/shard_map/all_gather | solution.py:172
  9.1 103.6 %all-gather.12.cloned.1.call-start = ((), (), s32[]{:S(2)}) async-start(), calls=%async_computation.8 | async-start | bytes 1114112 | tf_op jit(solution)/shard_map/all_gather | solution.py:173
  10.7 128.3 %all-gather.18.cloned.1.call-start = ((), (), s32[]{:S(2)}) async-start(), calls=%async_computation.17 | async-start | bytes 1572864 | tf_op jit(solution)/shard_map/all_gather | solution.py:201
  16.2 273.3 %copy-start.67 = (f32[1024]{0:T(1024)}, f32[1024]{0:T(1024)S(1)}, u32[]{:S(2)}) copy-start(f32[1024]{0:T(1024)S(1)} %fusion.227) | copy-start | bytes 12292
  17.5 55.2 %copy-start.59 = (f32[1,2048]{1,0:T(1,128)}, f32[1,2048]{1,0:T(1,128)S(1)}, u32[]{:S(2)}) copy-start(f32[1,2048]{1,0:T(1,128)S(1)} %get-tuple-element.676) | copy-start | bytes 24580
  17.5 55.2 %copy-start.71 = (f32[1,2048]{1,0:T(1,128)}, f32[1,2048]{1,0:T(1,128)S(1)}, u32[]{:S(2)}) copy-start(f32[1,2048]{1,0:T(1,128)S(1)} %get-tuple-element.675) | copy-start | bytes 24580
  73.3 6.8 copy-start.86
  80.0 10.2 copy-start.26
  80.1 85.8 %all-gather.10.cloned.1.call-start = ((), (), s32[]{:S(2)}) async-start(), calls=%async_computation.7 | async-start | bytes 1572864 | tf_op jit(solution)/shard_map/all_gather | solution.py:200
  90.1 133.9 %all-gather.16.cloned.1.call-start = ((), (), s32[]{:S(2)}) async-start(), calls=%async_computation.10 | async-start | bytes 4456448 | tf_op jit(solution)/shard_map/all_gather | solution.py:175
  91.0 190.7 %all-gather.14.cloned.1.call-start = ((), (), s32[]{:S(2)}) async-start(), calls=%async_computation.9 | async-start | bytes 4456448 | tf_op jit(solution)/shard_map/all_gather | solution.py:174
  91.8 239.5 %reduce-scatter.7.cloned.1.call-start = ((), (), s32[]{:S(2)}) async-start(), calls=%async_computation.11 | async-start | bytes 3145728 | tf_op jit(solution)/shard_map/reduce_scatter | solution.py:298
  118.1 6.8 copy-start.16
  128.1 40.0 %copy-start.76 = (f32[2,1,512]{2,1,0:T(1,128)S(1)}, f32[2,1,512]{2,1,0:T(1,128)}, u32[]{:S(2)}) copy-start(f32[2,1,512]{2,1,0:T(1,128)} %custom-call.18) | copy-start | bytes 12292
  178.8 21.8 %copy-start.74 = (f32[1,1792]{1,0:T(1,128)S(1)}, f32[1,1792]{1,0:T(1,128)}, u32[]{:S(2)}) copy-start(f32[1,1792]{1,0:T(1,128)} %param.49) | copy-start | bytes 21508
  178.8 22.4 %copy-start.85 = (s32[16]{0:T(128)S(1)}, s32[16]{0:T(128)}, u32[]{:S(2)}) copy-start(s32[16]{0:T(128)} %get-tuple-element.689) | copy-start | bytes 196
  178.8 22.4 %copy-start.84 = (s32[16]{0:T(128)S(1)}, s32[16]{0:T(128)}, u32[]{:S(2)}) copy-start(s32[16]{0:T(128)} %get-tuple-element.691) | copy-start | bytes 196
  200.5 155.9 %reduce-scatter.9.cloned.1.call-start = ((), (), s32[]{:S(2)}) async-start(), calls=%async_computation.12 | async-start | bytes 3145728 | tf_op jit(solution)/shard_map/reduce_scatter | solution.py:299
  205.8 23.6 %copy-start.83 = (pred[16]{0:T(512)(128)(4,1)S(1)}, pred[16]{0:T(512)(128)(4,1)}, u32[]{:S(2)}) copy-start(pred[16]{0:T(512)(128)(4,1)} %get-tuple-element.688) | copy-start | bytes 52
  205.8 1131.9 %all-reduce.9.cloned.1.call-start = ((), (), s32[]{:S(2)}) async-start(), calls=%async_computation.18 | async-start | bytes 50331648 | tf_op jit(solution)/shard_map/psum | solution.py:240
  240.6 46.1 %copy-start.82 = (pred[16]{0:T(512)(128)(4,1)S(1)}, pred[16]{0:T(512)(128)(4,1)}, u32[]{:S(2)}) copy-start(pred[16]{0:T(512)(128)(4,1)} %get-tuple-element.690) | copy-start | bytes 52
  290.2 15.2 copy-start.18
  324.3 8.2 copy-start.64
  366.3 1053.4 %reduce-scatter.13.cloned.1.call-start = ((), (), s32[]{:S(2)}) async-start(), calls=%async_computation.14 | async-start | bytes 2228224 | tf_op jit(solution)/shard_map/reduce_scatter | solution.py:356
  366.3 6.5 copy-start.80
  366.3 6.6 copy-start.32
  385.4 1140.1 %reduce-scatter.15.cloned.1.call-start = ((), (), s32[]{:S(2)}) async-start(), calls=%async_computation.15 | async-start | bytes 8912896 | tf_op jit(solution)/shard_map/reduce_scatter | solution.py:357
  413.8 1217.2 %reduce-scatter.17.cloned.1.call-start = ((), (), s32[]{:S(2)}) async-start(), calls=%async_computation.16 | async-start | bytes 8912896 | tf_op jit(solution)/shard_map/reduce_scatter | solution.py:358
  440.6 897.1 %copy-start.60 = (f32[1,2048]{1,0:T(1,128)S(1)}, f32[1,2048]{1,0:T(1,128)}, u32[]{:S(2)}) copy-start(f32[1,2048]{1,0:T(1,128)} %copy-done.59) | copy-start | bytes 24580
  440.6 1283.4 %reduce-scatter.11.cloned.1.call-start = ((), (), s32[]{:S(2)}) async-start(), calls=%async_computation.13 | async-start | bytes 6684672 | tf_op jit(solution)/shard_map/reduce_scatter | solution.py:355
  1337.7 11.9 slice-start
  1337.7 9.5 copy-start.66
  1337.7 11.9 copy-start.4
  1337.7 13.1 slice-start.1
  1337.7 13.1 copy-start.9
  1350.8 14.4 copy-start.11
  1350.8 14.4 copy-start.70
  1350.8 14.4 copy-start.72
  1350.8 14.4 copy-start.73
  1408.5 11.1 copy-start.42
  1408.5 12.4 copy-start.54
  1408.5 14.4 copy-start.46
  1408.5 53.5 %copy-start.75 = (f32[1,1792]{1,0:T(1,128)S(1)}, f32[1,1792]{1,0:T(1,128)}, u32[]{:S(2)}) copy-start(f32[1,1792]{1,0:T(1,128)} %param.49) | copy-start | bytes 21508
  1420.9 111.5 %copy-start.43 = (f32[1,128,1024]{2,1,0:T(8,128)S(1)}, f32[1,128,1024]{2,1,0:T(8,128)}, u32[]{:S(2)}) copy-start(f32[1,128,1024]{2,1,0:T(8,128)} %param.63) | copy-start | bytes 1572868
  1424.1 110.7 %copy-start.47 = (f32[256,128]{1,0:T(8,128)}, f32[256,128]{1,0:T(8,128)S(1)}, u32[]{:S(2)}) copy-start(f32[256,128]{1,0:T(8,128)S(1)} %fusion.129) | copy-start | bytes 393220
  1527.6 7.2 copy-start.13
  1527.6 7.2 copy-start.34
  1540.2 95.7 %copy-start.50 = (f32[1024,1,128]{2,1,0:T(1,128)S(1)}, f32[1024,1,128]{2,1,0:T(1,128)}, u32[]{:S(2)}) copy-start(f32[1024,1,128]{2,1,0:T(1,128)} %param.68) | copy-start | bytes 1572868
  1540.2 95.7 %copy-start.55 = (f32[1,1,128,128]{3,2,1,0:T(8,128)S(1)}, f32[1,1,128,128]{3,2,1,0:T(8,128)}, u32[]{:S(2)}) copy-start(f32[1,1,128,128]{3,2,1,0:T(8,128)} %param.71) | copy-start | bytes 196612
  1631.0 6.0 copy-start.14
  1636.0 6.0 copy-start.27
  1637.0 7.8 copy-start.36
  1637.0 7.8 copy-start.37
  1637.0 6.7 copy-start.44
  1637.0 6.7 copy-start.45
  1637.0 7.8 copy-start.61
  1637.1 7.8 copy-start.69
  1637.1 80.5 %copy-start.57 = (f32[6,2048]{1,0:T(8,128)S(1)}, f32[6,2048]{1,0:T(8,128)}, u32[]{:S(2)}) copy-start(f32[6,2048]{1,0:T(8,128)} %param.46) | copy-start | bytes 147460
  1642.9 86.6 %copy-start.28 = (f32[1024,128]{1,0:T(8,128)}, f32[1024,128]{1,0:T(8,128)S(1)}, u32[]{:S(2)}) copy-start(f32[1024,128]{1,0:T(8,128)S(1)} %fusion.122) | copy-start | bytes 1572868
  1643.0 84.4 %copy-start.62 = (f32[1,1,128,128]{3,2,1,0:T(8,128)S(1)}, f32[1,1,128,128]{3,2,1,0:T(8,128)}, u32[]{:S(2)}) copy-start(f32[1,1,128,128]{3,2,1,0:T(8,128)} %param.55) | copy-start | bytes 196612
  1719.1 11.4 copy-start.39
  1724.0 5.5 copy-start.52
  1724.0 5.5 copy-start.53
  (52 other events, 137.2 us)
Sparse Core Ops, SparseCore 0:
  11.0 54.8 all-gather.7
  68.9 43.7 all-gather.11
  114.9 24.0 all-gather.17
  141.1 24.6 all-gather.9
  168.7 55.2 all-gather.15
  226.9 54.7 all-gather.13
  284.0 34.6 reduce-scatter.6
  321.1 35.2 reduce-scatter.8
  366.4 971.2 all-reduce.8
  1341.5 78.0 reduce-scatter.12
  1424.0 101.5 reduce-scatter.14
  1529.8 101.2 reduce-scatter.16
  1635.2 88.8 reduce-scatter.10
where the time goes:
time: 1750 us; the launch traced here: 1740 us
  waiting for transfers between devices  1250 us (71%)
  matrix products  144 us (8%)
  local copies, waits for them, and re-layouts  110 us (6%)
  other arithmetic  109 us (6%)
  blocking collectives  108 us (6%)
  between operations  20.5 us (1%)
    psum x1, waiting for transfers between devices, per_device(): branches = lax.psum(partial_out, 'tp')  897 us
    reduce_scatter x1, waiting for transfers between devices, per_device(): lax.psum_scatter(slot_down, ('dp', 'sp'), scatter_dimension=1, tiled=True)  90.1 us
    psum x1, blocking collectives, per_device(): shared_grad = lax.psum(shared_part, ('dp', 'sp', 'tp'))  71.9 us
    reduce_scatter x1, waiting for transfers between devices, per_device(): lax.psum_scatter(slot_up, ('dp', 'sp'), scatter_dimension=0, tiled=True)  62.2 us
    all_gather x1, waiting for transfers between devices, per_device(): lax.all_gather(qkv_low, ('dp', 'sp'), axis=0, tiled=True)  48.4 us
    all_gather x1, waiting for transfers between devices, per_device(): lax.all_gather(up_low, ('dp', 'sp'), axis=0, tiled=True)  41.1 us
    dot_general x16, matrix products, exact_dot(): jnp.dot(left_matrix, right_matrix, precision=lax.Precision.HIGHEST, prefe...  37.4 us
    psum x1, blocking collectives, per_device(): split_grad = lax.psum(split_part, ('dp', 'sp'))  36.5 us
  transfers between devices with their start and end apart: 13, of which 12 were waited for; matrix products, arithmetic and copies ran while one was open for 19% of the time, Pallas kernels for 0%

commit v1 on v0

v1 whole, which is shorter than its diff:
```python
import jax
import jax.numpy as jnp
from jax import lax
from jax.experimental import pallas as pl
from jax.experimental.pallas import tpu as pltpu
from jax.sharding import Mesh, PartitionSpec as P

D = 2048
H = 8
STEP = 5


ln_eps = 1e-05
adam_eps = 1e-08
beta_one = 0.5
beta_two = 0.5
rate_qkv = 0.01
rate_out = 0.05
rate_up = 0.01
rate_down = 0.005
rate_vector = 0.2
weight_decay = 0.01


def exact_dot(left_matrix, right_matrix):
    return jnp.dot(
        left_matrix,
        right_matrix,
        precision=lax.Precision.HIGHEST,
        preferred_element_type=jnp.float32,
    )


def contract_rows(left_matrix, right_matrix):
    return lax.dot_general(
        left_matrix, right_matrix, (((0,), (0,)), ((), ())), preferred_element_type=jnp.float32
    )


def contract_cols(left_matrix, right_matrix):
    return lax.dot_general(
        left_matrix, right_matrix, (((1,), (1,)), ((), ())), preferred_element_type=jnp.float32
    )


def layer_norm(field, gain, shift):
    center = field - jnp.mean(field, axis=-1, keepdims=True)
    spread = jnp.mean(center * center, axis=-1, keepdims=True)
    return center * lax.rsqrt(spread + ln_eps) * gain + shift


def gelu_exact(field):
    return jax.nn.gelu(field, approximate=False)


def rotate(field, places, rot_dims):
    half_dims = rot_dims // 2
    frequency = 10000.0 ** (-2.0 * jnp.arange(half_dims, dtype=jnp.float32) / rot_dims)
    angles = places.astype(jnp.float32)[:, None] * frequency[None, :]
    cosine = jnp.cos(angles)[:, None, :]
    sine_part = jnp.sin(angles)[:, None, :]
    front = field[..., :half_dims]
    middle = field[..., half_dims:rot_dims]
    return jnp.concatenate(
        [
            front * cosine - middle * sine_part,
            middle * cosine + front * sine_part,
            field[..., rot_dims:],
        ],
        axis=-1,
    )


def row_places(first_len, second_len, part_index, local_index, part_count):
    first_rows = first_len // part_count
    in_first = local_index < first_rows
    segment = jnp.where(in_first, 0, 1).astype(jnp.int32)
    position = jnp.where(
        in_first,
        part_index * first_rows + local_index,
        part_index * (second_len // part_count) + local_index - first_rows,
    )
    return (segment, position)


def soap_block(gradient, weight, first_moment, second_moment, left_basis, right_basis, step_rate):
    turned = exact_dot(exact_dot(left_basis.T, gradient), right_basis)
    first_new = beta_one * first_moment + (1.0 - beta_one) * turned
    second_new = beta_two * second_moment + (1.0 - beta_two) * turned * turned
    direction = (
        first_new
        / (1.0 - beta_one**STEP)
        / (jnp.sqrt(second_new / (1.0 - beta_two**STEP)) + adam_eps)
    )
    returned = exact_dot(exact_dot(left_basis, direction), right_basis.T)
    return (weight * (1.0 - step_rate * weight_decay) - step_rate * returned, first_new, second_new)


def adam_vector(gradient, current, first_moment, second_moment):
    first_new = beta_one * first_moment + (1.0 - beta_one) * gradient
    second_new = beta_two * second_moment + (1.0 - beta_two) * gradient * gradient
    direction = (
        first_new
        / (1.0 - beta_one**STEP)
        / (jnp.sqrt(second_new / (1.0 - beta_two**STEP)) + adam_eps)
    )
    return (current - rate_vector * direction, first_new, second_new)


UP = [(i, (i + 1) % 4) for i in range(4)]
DOWN = [(i, (i + 3) % 4) for i in range(4)]
PAIR = [(0, 1), (1, 0)]
bf16 = jnp.bfloat16
f32 = jnp.float32


def relative_slots():
    y, c, s = lax.axis_index("y"), lax.axis_index("c"), lax.axis_index("s")
    r = jnp.arange(16, dtype=jnp.int32)
    core = c ^ (r // 8)
    row = (y + (r // 2) % 4) % 4
    part = s ^ (r % 2)
    return (row * 2 + core) * 2 + part


def place_blocks(places, sources, plan, out_shape, columns):
    block = sources[0].shape[1:]

    def kernel(place_ref, *refs):
        ins, out, hold, in_sems, out_sems = refs[:-4], refs[-4], refs[-3], refs[-2], refs[-1]
        inward, outward = [], []
        for k, (which, part) in enumerate(plan):
            if columns:
                start = pl.multiple_of(place_ref[k] * block[1], block[1])
                target = out.at[:, pl.ds(start, block[1])]
            else:
                start = pl.multiple_of(place_ref[k] * block[0], block[0])
                target = out.at[pl.ds(start, block[0])]
            inward.append(pltpu.make_async_copy(ins[which].at[part], hold.at[k], in_sems.at[k]))
            outward.append(pltpu.make_async_copy(hold.at[k], target, out_sems.at[k]))
        for copy in inward:
            copy.start()
        for first, second in zip(inward, outward):
            first.wait()
            second.start()
        for copy in outward:
            copy.wait()

    return pl.pallas_call(
        kernel,
        out_shape=jax.ShapeDtypeStruct(out_shape, sources[0].dtype),
        in_specs=[pl.BlockSpec(memory_space=pltpu.SMEM)]
        + [pl.BlockSpec(memory_space=pl.ANY)] * len(sources),
        out_specs=pl.BlockSpec(memory_space=pl.ANY),
        scratch_shapes=[
            pltpu.VMEM((len(plan), *block), sources[0].dtype),
            pltpu.SemaphoreType.DMA((len(plan),)),
            pltpu.SemaphoreType.DMA((len(plan),)),
        ],
        compiler_params=pltpu.CompilerParams(vmem_limit_bytes=32 * 2**20),
    )(places, *sources)


def pick_blocks(places, field, out_shape, columns):
    amount = out_shape[0]
    block = out_shape[1:]

    def kernel(place_ref, field_ref, out, hold, in_sems, out_sems):
        inward, outward = [], []
        for k in range(amount):
            if columns:
                start = pl.multiple_of(place_ref[k] * block[1], block[1])
                origin = field_ref.at[:, pl.ds(start, block[1])]
            else:
                start = pl.multiple_of(place_ref[k] * block[0], block[0])
                origin = field_ref.at[pl.ds(start, block[0])]
            inward.append(pltpu.make_async_copy(origin, hold.at[k], in_sems.at[k]))
            outward.append(pltpu.make_async_copy(hold.at[k], out.at[k], out_sems.at[k]))
        for copy in inward:
            copy.start()
        for first, second in zip(inward, outward):
            first.wait()
            second.start()
        for copy in outward:
            copy.wait()

    return pl.pallas_call(
        kernel,
        out_shape=jax.ShapeDtypeStruct(out_shape, field.dtype),
        in_specs=[pl.BlockSpec(memory_space=pltpu.SMEM), pl.BlockSpec(memory_space=pl.ANY)],
        out_specs=pl.BlockSpec(memory_space=pl.ANY),
        scratch_shapes=[
            pltpu.VMEM(out_shape, field.dtype),
            pltpu.SemaphoreType.DMA((amount,)),
            pltpu.SemaphoreType.DMA((amount,)),
        ],
        compiler_params=pltpu.CompilerParams(vmem_limit_bytes=32 * 2**20),
    )(places, field)


def fetch(block):
    pair = jnp.concatenate([block, lax.ppermute(block, "s", PAIR)], axis=0)
    before = lax.ppermute(pair, "y", UP)
    after = lax.ppermute(pair, "y", DOWN)
    far_a = lax.ppermute(before[0:1], "y", UP)
    far_b = lax.ppermute(after[1:2], "y", DOWN)
    half = jnp.concatenate([pair, after, far_a, far_b, before], axis=0)
    other = lax.ppermute(half, "c", PAIR)
    return [half, other]


FETCH_PLAN = [(k // 8, k % 8) for k in range(16)]


def deliver(blocks):
    sibling = lax.ppermute(blocks[8:], "c", PAIR)

    def both(low, high):
        return blocks[low:high].astype(f32) + sibling[low:high].astype(f32)

    far_a = lax.ppermute(both(4, 5).astype(bf16), "y", UP)
    far_b = lax.ppermute(both(5, 6).astype(bf16), "y", DOWN)
    to_next = jnp.concatenate([both(2, 3) + far_a.astype(f32), both(3, 4)], axis=0).astype(bf16)
    to_prev = jnp.concatenate([both(6, 7), both(7, 8) + far_b.astype(f32)], axis=0).astype(bf16)
    from_prev = lax.ppermute(to_next, "y", UP)
    from_next = lax.ppermute(to_prev, "y", DOWN)
    total = both(0, 2) + from_prev.astype(f32) + from_next.astype(f32)
    partner = lax.ppermute(total[1:2].astype(bf16), "s", PAIR)
    return total[0] + partner[0].astype(f32)


def tp_sum_rows(partial):
    x, z = lax.axis_index("x"), lax.axis_index("z")

    def rows(offset, low, size):
        start = ((x + offset) % 4) * 256 + low
        return lax.dynamic_slice_in_dim(partial, start, size, axis=0).astype(f32)

    far_a = lax.ppermute(rows(2, 0, 128).astype(bf16), "x", UP)
    far_b = lax.ppermute(rows(2, 128, 128).astype(bf16), "x", DOWN)
    to_next = jnp.concatenate([rows(1, 0, 128) + far_a.astype(f32), rows(1, 128, 128)], axis=0).astype(bf16)
    to_prev = jnp.concatenate([rows(3, 0, 128), rows(3, 128, 128) + far_b.astype(f32)], axis=0).astype(bf16)
    from_prev = lax.ppermute(to_next, "x", UP)
    from_next = lax.ppermute(to_prev, "x", DOWN)

    def total(start):
        own = lax.dynamic_slice_in_dim(partial, x * 256 + start, 128, axis=0).astype(f32)
        one = lax.dynamic_slice_in_dim(from_prev, start, 128, axis=0).astype(f32)
        two = lax.dynamic_slice_in_dim(from_next, start, 128, axis=0).astype(f32)
        return own + one + two

    partner = lax.ppermute(total((1 - z) * 128).astype(bf16), "z", PAIR)
    return total(z * 128) + partner.astype(f32)


def tp_gather_rows(rows):
    x, z = lax.axis_index("x"), lax.axis_index("z")
    partner = lax.ppermute(rows, "z", PAIR)
    low = jnp.where(z == 0, rows, partner)
    high = jnp.where(z == 0, partner, rows)
    pair = jnp.stack([low, high])
    before = lax.ppermute(pair, "x", UP)
    after = lax.ppermute(pair, "x", DOWN)
    far_a = lax.ppermute(before[0:1], "x", UP)
    far_b = lax.ppermute(after[1:2], "x", DOWN)
    steps = jnp.array([0, 0, 1, 1, 2, 2, 3, 3], jnp.int32)
    places = ((x + steps) % 4) * 2 + jnp.arange(8, dtype=jnp.int32) % 2
    plan = [(0, 0), (0, 1), (1, 0), (1, 1), (2, 0), (3, 0), (4, 0), (4, 1)]
    return place_blocks(
        places, [pair, after, far_a, far_b, before], plan, (1024, rows.shape[1]), False
    )


def exchange_add(vector, axis, order):
    return vector + lax.ppermute(vector, axis, order)


def per_device(
    tokens,
    cotangent,
    seq_lens,
    owners,
    shared_vec,
    shared_first,
    shared_second,
    split_vec,
    split_first,
    split_second,
    qkv_master,
    qkv_first,
    qkv_second,
    qkv_left,
    qkv_right,
    out_master,
    out_first,
    out_second,
    out_left,
    out_right,
    up_master,
    up_first,
    up_second,
    up_left,
    up_right,
    down_master,
    down_first,
    down_second,
    down_left,
    down_right,
):
    row_count = tokens.shape[0]
    head_size = D // H
    qkv_cols = qkv_master.shape[2]
    sp_rank = lax.axis_index("s")
    x, z = lax.axis_index("x"), lax.axis_index("z")
    tp_rank = x * 2 + z
    scale = head_size ** (-0.5)
    rot_dims = head_size // 4
    slots = relative_slots()
    block_ids = jnp.arange(16, dtype=jnp.int32)
    places = jnp.sum(
        jnp.where(owners[:, None, :] == slots[None, :, None], block_ids[None, None, :], 0), axis=2
    )
    qkv_low = qkv_master.astype(bf16)
    out_low = out_master.astype(bf16).reshape(1, 256, 128)
    up_low = up_master.astype(bf16)
    down_low = down_master.astype(bf16).reshape(1, 1024, 128)
    w_qkv = place_blocks(places[0], fetch(qkv_low), FETCH_PLAN, (2048, 768), False)
    w_out = place_blocks(places[1], fetch(out_low), FETCH_PLAN, (256, 2048), True)
    w_up = place_blocks(places[2], fetch(up_low), FETCH_PLAN, (2048, 1024), False)
    w_down = place_blocks(places[3], fetch(down_low), FETCH_PLAN, (1024, 2048), True)
    field = tokens.astype(f32)
    center = field - jnp.mean(field, axis=-1, keepdims=True)
    inverse_std = lax.rsqrt(jnp.mean(center * center, axis=-1, keepdims=True) + ln_eps)
    unit = center * inverse_std
    h_one = (unit * shared_vec[0] + shared_vec[1]).astype(bf16)
    h_two = (unit * shared_vec[2] + shared_vec[3]).astype(bf16)
    b_qkv = split_vec[0, :qkv_cols]
    b_up = split_vec[0, qkv_cols:]
    qkv_raw = jnp.dot(h_one, w_qkv, preferred_element_type=f32) + b_qkv
    local_index = jnp.arange(row_count, dtype=jnp.int32)
    query_seg, query_pos = row_places(seq_lens[0, 0], seq_lens[0, 1], sp_rank, local_index, 2)
    far_seg, far_pos = row_places(seq_lens[0, 0], seq_lens[0, 1], 0, local_index, 2)
    far_seg = jnp.where(sp_rank == 1, far_seg, 2)

    def turned(values_in):
        return rotate(values_in[:, None, :], query_pos, rot_dims)[:, 0]

    query_raw = qkv_raw[:, :256]
    key_raw = qkv_raw[:, 256:512]
    query_low = turned(query_raw).astype(bf16)
    key_low = turned(key_raw).astype(bf16)
    value_low = qkv_raw[:, 512:].astype(bf16)
    far_kv = lax.ppermute(jnp.stack([key_low, value_low]), "s", [(0, 1)])
    key_all = jnp.concatenate([key_low, far_kv[0]], axis=0)
    value_all = jnp.concatenate([value_low, far_kv[1]], axis=0)
    key_seg = jnp.concatenate([query_seg, far_seg])
    key_pos = jnp.concatenate([query_pos, far_pos])
    visible = (query_seg[:, None] == key_seg[None, :]) & (key_pos[None, :] <= query_pos[:, None])
    scores = contract_cols(query_low, key_all) * scale
    scores = jnp.where(visible, scores, -1e30)
    maximum = jnp.max(scores, axis=-1, keepdims=True)
    exponent = jnp.exp(scores - maximum)
    denominator = jnp.sum(exponent, axis=-1, keepdims=True)
    probability = exponent / denominator
    prob_low = probability.astype(bf16)
    attended_low = jnp.dot(prob_low, value_all, preferred_element_type=f32).astype(bf16)
    grad_attended = contract_cols(cotangent, w_out).astype(bf16)
    grad_probs = contract_cols(grad_attended, value_all)
    inner = jnp.sum(grad_probs * probability, axis=-1, keepdims=True)
    grad_scores = (probability * (grad_probs - inner) * scale).astype(bf16)
    grad_query = jnp.dot(grad_scores, key_all, preferred_element_type=f32)
    key_sum = contract_rows(grad_scores, query_low)
    value_sum = contract_rows(prob_low, grad_attended)
    far_grads = lax.ppermute(
        jnp.stack([key_sum[row_count:], value_sum[row_count:]]).astype(bf16), "s", [(1, 0)]
    ).astype(f32)
    grad_key = key_sum[:row_count] + far_grads[0]
    grad_value = value_sum[:row_count] + far_grads[1]
    query_back = jax.vjp(turned, query_raw)[1]
    key_back = jax.vjp(turned, key_raw)[1]
    grad_qkv = jnp.concatenate(
        [query_back(grad_query)[0], key_back(grad_key)[0], grad_value], axis=1
    ).astype(bf16)

    pre_act = jnp.dot(h_two, w_up, preferred_element_type=f32) + b_up
    hidden_low = gelu_exact(pre_act).astype(bf16)
    partial_out = (
        jnp.dot(attended_low, w_out, preferred_element_type=f32)
        + jnp.dot(hidden_low, w_down, preferred_element_type=f32)
    ).astype(bf16)
    own_start = tp_rank * 128

    def own(values_in):
        return lax.dynamic_slice_in_dim(values_in, own_start, 128, axis=0)

    branches = tp_sum_rows(partial_out)
    output = tp_gather_rows(
        (own(tokens).astype(f32) + branches + shared_vec[4] + shared_vec[5]).astype(bf16)
    )
    grad_hidden = contract_cols(cotangent, w_down)
    gelu_back = jax.vjp(gelu_exact, pre_act)[1]
    grad_pre = gelu_back(grad_hidden)[0].astype(bf16)
    grad_h_two = contract_cols(grad_pre, w_up)
    grad_h_one = contract_cols(grad_qkv, w_qkv)
    grad_unit = (grad_h_one * shared_vec[0] + grad_h_two * shared_vec[2]).astype(bf16)
    own_grad = tp_sum_rows(grad_unit)
    own_field = own(tokens).astype(f32)
    own_center = own_field - jnp.mean(own_field, axis=-1, keepdims=True)
    own_inverse = lax.rsqrt(jnp.mean(own_center * own_center, axis=-1, keepdims=True) + ln_eps)
    own_unit = own_center * own_inverse
    grad_x = (
        own_grad
        - jnp.mean(own_grad, axis=-1, keepdims=True)
        - own_unit * jnp.mean(own_grad * own_unit, axis=-1, keepdims=True)
    ) * own_inverse
    grad_input = tp_gather_rows((own(cotangent).astype(f32) + grad_x).astype(bf16))

    bias_share = jnp.sum(cotangent.astype(f32), axis=0) * 0.125
    shared_part = jnp.stack(
        [
            jnp.sum(grad_h_one * unit, axis=0),
            jnp.sum(grad_h_one, axis=0),
            jnp.sum(grad_h_two * unit, axis=0),
            jnp.sum(grad_h_two, axis=0),
            bias_share,
        ]
    )
    split_part = jnp.concatenate(
        [jnp.sum(grad_qkv.astype(f32), axis=0), jnp.sum(grad_pre.astype(f32), axis=0)]
    )
    sums = jnp.concatenate([shared_part.reshape(80, 128), split_part.reshape(14, 128)], axis=0)
    sums = exchange_add(sums, "c", PAIR)
    sums = exchange_add(sums, "s", PAIR)
    sums = exchange_add(sums, "y", [(i, i ^ 1) for i in range(4)])
    sums = exchange_add(sums, "y", [(i, i ^ 2) for i in range(4)])
    split_grad = sums[80:].reshape(1, 1792)
    shared_sum = exchange_add(sums[:80], "z", PAIR)
    shared_sum = exchange_add(shared_sum, "x", [(i, i ^ 1) for i in range(4)])
    shared_sum = exchange_add(shared_sum, "x", [(i, i ^ 2) for i in range(4)])
    shared_sum = shared_sum.reshape(5, 2048)
    shared_grad = jnp.concatenate([shared_sum, shared_sum[4:5]], axis=0)

    grad_out_w = contract_rows(attended_low, cotangent).astype(bf16)
    grad_down_w = contract_rows(hidden_low, cotangent).astype(bf16)
    grad_up_w = contract_rows(h_two, grad_pre).astype(bf16)
    grad_qkv_w = contract_rows(h_one, grad_qkv).astype(bf16)
    sum_qkv = deliver(pick_blocks(places[0], grad_qkv_w, (16, 128, 768), False))
    sum_out = deliver(pick_blocks(places[1], grad_out_w, (16, 256, 128), True))
    sum_up = deliver(pick_blocks(places[2], grad_up_w, (16, 128, 1024), False))
    sum_down = deliver(pick_blocks(places[3], grad_down_w, (16, 1024, 128), True))
    new_qkv = soap_block(
        sum_qkv,
        qkv_master[0],
        qkv_first[0],
        qkv_second[0],
        qkv_left[0, 0],
        qkv_right[0, 0],
        rate_qkv,
    )
    new_out = soap_block(
        sum_out,
        out_master[:, 0],
        out_first[:, 0],
        out_second[:, 0],
        out_left[0, 0],
        out_right[0, 0],
        rate_out,
    )
    new_up = soap_block(
        sum_up, up_master[0], up_first[0], up_second[0], up_left[0, 0], up_right[0, 0], rate_up
    )
    new_down = soap_block(
        sum_down,
        down_master[:, 0],
        down_first[:, 0],
        down_second[:, 0],
        down_left[0, 0],
        down_right[0, 0],
        rate_down,
    )
    new_shared = adam_vector(shared_grad, shared_vec, shared_first, shared_second)
    new_split = adam_vector(split_grad, split_vec, split_first, split_second)
    return (
        output,
        grad_input,
        new_shared[0],
        new_shared[1],
        new_shared[2],
        new_split[0],
        new_split[1],
        new_split[2],
        new_qkv[0][None],
        new_qkv[1][None],
        new_qkv[2][None],
        new_qkv[0][None].astype(bf16),
        new_out[0][:, None],
        new_out[1][:, None],
        new_out[2][:, None],
        new_out[0][:, None].astype(bf16),
        new_up[0][None],
        new_up[1][None],
        new_up[2][None],
        new_up[0][None].astype(bf16),
        new_down[0][:, None],
        new_down[1][:, None],
        new_down[2][:, None],
        new_down[0][:, None].astype(bf16),
    )


def solution(mesh):
    in_specs = (
        P(("y", "c", "s"), None),
        P(("y", "c", "s"), None),
        P(("y", "c"), None),
        P(),
        P(),
        P(),
        P(),
        P(("x", "z"), None),
        P(("x", "z"), None),
        P(("x", "z"), None),
        P(("y", "c", "s"), None, ("x", "z")),
        P(("y", "c", "s"), None, ("x", "z")),
        P(("y", "c", "s"), None, ("x", "z")),
        P(("y", "c", "s"), ("x", "z"), None, None),
        P(("y", "c", "s"), ("x", "z"), None, None),
        P(("x", "z"), ("y", "c", "s"), None),
        P(("x", "z"), ("y", "c", "s"), None),
        P(("x", "z"), ("y", "c", "s"), None),
        P(("y", "c", "s"), ("x", "z"), None, None),
        P(("y", "c", "s"), ("x", "z"), None, None),
        P(("y", "c", "s"), None, ("x", "z")),
        P(("y", "c", "s"), None, ("x", "z")),
        P(("y", "c", "s"), None, ("x", "z")),
        P(("y", "c", "s"), ("x", "z"), None, None),
        P(("y", "c", "s"), ("x", "z"), None, None),
        P(("x", "z"), ("y", "c", "s"), None),
        P(("x", "z"), ("y", "c", "s"), None),
        P(("x", "z"), ("y", "c", "s"), None),
        P(("y", "c", "s"), ("x", "z"), None, None),
        P(("y", "c", "s"), ("x", "z"), None, None),
    )
    out_specs = (
        P(("y", "c", "s"), None),
        P(("y", "c", "s"), None),
        P(),
        P(),
        P(),
        P(("x", "z"), None),
        P(("x", "z"), None),
        P(("x", "z"), None),
        P(("y", "c", "s"), None, ("x", "z")),
        P(("y", "c", "s"), None, ("x", "z")),
        P(("y", "c", "s"), None, ("x", "z")),
        P(("y", "c", "s"), None, ("x", "z")),
        P(("x", "z"), ("y", "c", "s"), None),
        P(("x", "z"), ("y", "c", "s"), None),
        P(("x", "z"), ("y", "c", "s"), None),
        P(("x", "z"), ("y", "c", "s"), None),
        P(("y", "c", "s"), None, ("x", "z")),
        P(("y", "c", "s"), None, ("x", "z")),
        P(("y", "c", "s"), None, ("x", "z")),
        P(("y", "c", "s"), None, ("x", "z")),
        P(("x", "z"), ("y", "c", "s"), None),
        P(("x", "z"), ("y", "c", "s"), None),
        P(("x", "z"), ("y", "c", "s"), None),
        P(("x", "z"), ("y", "c", "s"), None),
    )
    fine = Mesh(mesh.devices.reshape(4, 2, 2, 4, 2), ("y", "c", "s", "x", "z"))
    return jax.shard_map(
        per_device, mesh=fine, in_specs=in_specs, out_specs=out_specs, check_vma=False
    )
```

time: 1750 us -> 543 us (0.31)
  waiting for transfers between devices: 1250 us -> 155 us
  blocking collectives: 108 us -> 0 us
  starting transfers between devices: 1.59 us -> 105 us
  local copies, waits for them, and re-layouts: 110 us -> 29.3 us
  Pallas kernels: 0 us -> 38.2 us
  other arithmetic: 109 us -> 72.6 us
  matrix products: 144 us -> 125 us
    psum x1 -> x0, waiting for transfers between devices: 897 us -> none  [per_device(): branches = lax.psum(partial_out, 'tp')]
    reduce_scatter x6 -> x0, waiting for transfers between devices: 189 us -> none  [the longest x1 90.1 us: per_device(): lax.psum_scatter(slot_down, ('dp', 'sp'), scatter_dimension=1, tiled=True)]
    all_gather x6 -> x0, waiting for transfers between devices: 161 us -> none  [the longest x1 48.4 us: per_device(): lax.all_gather(qkv_low, ('dp', 'sp'), axis=0, tiled=True)]
    ppermute x0 -> x77, waiting for transfers between devices: none -> 155 us  [the longest x4 29.2 us: deliver(): far_a = lax.ppermute(both(4, 5).astype(bf16), 'y', UP)]
    psum x2 -> x0, blocking collectives: 108 us -> none  [the longest x1 71.9 us: per_device(): shared_grad = lax.psum(shared_part, ('dp', 'sp', 'tp'))]
    ppermute x0 -> x77, starting transfers between devices: none -> 105 us  [the longest x4 13.7 us: fetch(): far_b = lax.ppermute(after[1:2], 'y', DOWN)]
    gather x8 -> x0, local copies, waits for them, and re-layouts: 42.4 us -> none  [the longest x1 7.83 us: per_device(): jnp.take(grad_up_w.reshape(group_count, -1, grad_up_w.shape[1]), inverse_...]
    pallas_call x0 -> x10, Pallas kernels: none -> 38.2 us  [the longest x6 21.8 us: place_blocks(): pl.pallas_call(kernel, out_shape=jax.ShapeDtypeStruct(out_shape, sources[...]
  transfers between devices with their start and end apart: 13 -> 77, of which waited for: 12 -> 28; matrix products, arithmetic and copies ran while one was open for 19% -> 41% of each run, Pallas kernels for 0% -> 7%
where the time goes in v1:
time: 543 us; the launch traced here: 534 us
  waiting for transfers between devices  155 us (29%)
  matrix products  125 us (23%)
  starting transfers between devices  105 us (19%)
  other arithmetic  72.6 us (13%)
  Pallas kernels  38.2 us (7%)
  local copies, waits for them, and re-layouts  29.3 us (5%)
  between operations  8.12 us (1%)
    dot_general x6, matrix products, contract_cols(): lax.dot_general(left_matrix, right_matrix, (((1,), (1,)), ((), ())), pref...  38.8 us
    ppermute x4, waiting for transfers between devices, deliver(): far_a = lax.ppermute(both(4, 5).astype(bf16), 'y', UP)  29.2 us
    ppermute x2, waiting for transfers between devices, tp_gather_rows(): before = lax.ppermute(pair, 'x', UP)  29.1 us
    dot_general x16, matrix products, exact_dot(): jnp.dot(left_matrix, right_matrix, precision=lax.Precision.HIGHEST, prefe...  28 us
    dot_general x6, matrix products, contract_rows(): lax.dot_general(left_matrix, right_matrix, (((0,), (0,)), ((), ())), pref...  25.7 us
    pallas_call x6, Pallas kernels, place_blocks(): pl.pallas_call(kernel, out_shape=jax.ShapeDtypeStruct(out_shape, sources[...  21.8 us
    ppermute x7, waiting for transfers between devices, exchange_add(): return vector + lax.ppermute(vector, axis, order)  19.6 us
    pallas_call x4, Pallas kernels, pick_blocks(): pl.pallas_call(kernel, out_shape=jax.ShapeDtypeStruct(out_shape, field.dt...  16.4 us
  transfers between devices with their start and end apart: 77, of which 28 were waited for; matrix products, arithmetic and copies ran while one was open for 41% of the time, Pallas kernels for 7%

profile of v1, /device:TPU:0, one launch (start us, length us, event | category | flops | bytes accessed | tf_op | source)
XLA Modules:
  0.0 533.5 jit_solution(597141112275204445)
XLA Ops:
  2.4 4.0 collective-permute-start.7
  10.0 3.5 collective-permute-start.19
  22.6 2.8 convert_reduce_fusion
  29.4 3.8 fusion.12
  42.3 2.6 collective-permute-done.9
  47.0 2.9 collective-permute-start.11
  53.5 3.2 collective-permute-start.1
  57.9 3.3 collective-permute-start.20
  66.4 3.8 collective-permute-start.4
  70.9 6.0 %collective-permute-done.3 = bf16[1,128,768]{2,1,0:T(8,128)(2,1)S(1)} collective-permute-done((bf16[1,128,768]{2,1,0:T(8,128)(2,1)S(1)}, bf16[1,128,768]{2,1,0:T(8,128)(2,1)S(1)}, u32[]{:S(2)}, u32[]{:S(2)}) %collective-permute-start.3) | collective-permute-done | bytes 196640 | tf_op jit(solution)/shard_map/ppermute | solution.py:205
  79.4 3.8 collective-permute-start.14
  83.5 2.6 shard_map.488
  88.2 3.3 collective-permute-start.23
  91.6 3.8 collective-permute-done.14
  95.4 3.8 collective-permute-start.17
  101.3 5.0 collective-permute-done.17
  106.4 9.0 %shard_map.487 = bf16[2048,768]{1,0:T(8,128)(2,1)S(1)} custom-call(s32[16]{0:T(128)S(1)} %get-tuple-element.166.place_ref, bf16[8,128,768]{2,1,0:T(8,128)(2,1)S(1)} %copy-done.9, bf16[8,128,768]{2,1,0:T(8,128)(2,1)S(1)} %collective-permute-done.5.refs_1_), custom_call_target="tpu_custom_call" | custom-call | tf_op jit(solution)/shard_map/pallas_call | solution.py:149
  115.5 4.1 convolution_add_fusion
  122.5 5.2 collective-permute-start.6
  130.2 15.4 %multiply_convert_fusion.1 = (bf16[1024,1024]{1,0:T(8,128)(2,1)S(1)}, f32[1024,1024]{1,0:T(8,128)}, f32[1024,1024]{1,0:T(8,128)}) fusion(f32[1024]{0:T(1024)S(1)} %bitcast.328, bf16[2048,1024]{1,0:T(8,128)(2,1)S(1)} %shard_map.489, bf16[1024,2048]{1,0:T(8,128)(2,1)S(1)} %copy-done.10, f32[2048]{0:T(1024)S(1)} %bitcast.322, f32[2048]{0:T(1024)S(1)} %bitcast.319, ...), kind=kOutput, calls=%fused_computation.44 | convolution fusion | flops 4376756224 | bytes 18903040 | tf_op jit(solution)/shard_map/dot_general | solution.py:385
  148.0 10.2 %convert_reduce_fusion.2 = (f32[1024]{0:T(1024)}, bf16[1024,1024]{1,0:T(8,128)(2,1)S(1)}) fusion(f32[1024,1024]{1,0:T(8,128)} %get-tuple-element.94, bf16[1024,2048]{1,0:T(8,128)(2,1)S(1)} %shard_map.490, bf16[1024,2048]{1,0:T(8,128)(2,1)} %param.33, f32[1024,1024]{1,0:T(8,128)} %get-tuple-element.172, f32[1024]{0:T(1024)S(1)} %bitcast.329), kind=kOutput, calls=%fused_computation.43 | convolution fusion | flops 4312792064 | bytes 18882560 | tf_op jit(solution)/shard_map/dot_general | solution.py:41
  158.3 5.4 %convolution_convert_fusion.1.field_ref = bf16[2048,1024]{1,0:T(8,128)(2,1)S(1)} fusion(bf16[1024,1024]{1,0:T(8,128)(2,1)S(1)} %get-tuple-element.177, bf16[1024,2048]{1,0:T(8,128)(2,1)S(1)} %copy-done.10, f32[2048]{0:T(1024)S(1)} %bitcast.323, f32[2048]{0:T(1024)S(1)} %bitcast.320, f32[1024]{0:T(1024)S(1)} %copy-done.72, f32[1024]{0:T(1024)S(1)} %broadcast_multiply_fusion.1), kind=kOutput, calls=%fused_computation.59 | convolution fusion | flops 4309647360 | bytes 10510336 | tf_op jit(solution)/shard_map/dot_general | solution.py:35
  167.8 7.2 %convolution_convert_fusion.field_ref = bf16[1024,2048]{1,0:T(8,128)(2,1)S(1)} fusion(bf16[1024,1024]{1,0:T(8,128)(2,1)S(1)} %get-tuple-element.93, bf16[1024,2048]{1,0:T(8,128)(2,1)} %param.33), kind=kOutput, calls=%fused_computation.58 | convolution fusion | flops 4297064448 | bytes 10485760 | tf_op jit(solution)/shard_map/dot_general | solution.py:35
  179.1 6.8 %fusion.228 = f32[1024,2048]{1,0:T(8,128)} fusion(bf16[1024,1024]{1,0:T(8,128)(2,1)S(1)} %get-tuple-element.93, bf16[1024,2048]{1,0:T(8,128)(2,1)S(1)} %shard_map.490), kind=kOutput, calls=%fused_computation.422 | convolution fusion | flops 4294967296 | bytes 14680064 | tf_op jit(solution)/shard_map/dot_general | solution.py:389
  191.7 7.0 %multiply_reduce_fusion = (f32[1024]{0:T(1024)S(1)}, f32[1024,2048]{1,0:T(8,128)S(1)}, f32[1024,2048]{1,0:T(8,128)}) fusion(f32[1024]{0:T(1024)S(1)} %fusion.14, f32[1024,2048]{1,0:T(8,128)} %copy-done.15, f32[1024]{0:T(1024)S(1)} %get-tuple-element.173, bf16[256,1024]{1,0:T(8,128)(2,1)S(1)} %copy-done.40, bf16[1024,256]{0,1:T(8,128)(2,1)S(1)} %get-tuple-element.147, ...), kind=kOutput, calls=%fused_computation.18 | convolution fusion | flops 1084226560 | bytes 26750976 | tf_op jit(solution)/shard_map/dot_general | solution.py:41
  201.2 5.9 %multiply_convert_fusion = bf16[1024,2048]{1,0:T(8,128)(2,1)} fusion(f32[1024,2048]{1,0:T(8,128)S(1)} %get-tuple-element.86, f32[1024,2048]{1,0:T(8,128)} %get-tuple-element.175, f32[1024]{0:T(1024)S(1)} %get-tuple-element.85), kind=kLoop, calls=%fused_computation.17 | loop fusion | flops 8388608 | bytes 20975616 | tf_op jit(solution)/shard_map/convert_element_type | solution.py:370
  207.1 3.6 convolution_bitcast_fusion
  210.8 3.6 fusion.122
  226.8 9.6 %collective-permute-done.25 = bf16[128,2048]{1,0:T(8,128)(2,1)S(1)} collective-permute-done((bf16[128,2048]{1,0:T(8,128)(2,1)S(1)}, bf16[128,2048]{1,0:T(8,128)(2,1)S(1)}, u32[]{:S(2)}, u32[]{:S(2)}) %collective-permute-start.25) | collective-permute-done | bytes 524320 | tf_op jit(solution)/shard_map/ppermute | solution.py:239
  236.9 5.5 %collective-permute-done.60 = bf16[1,256,128]{2,1,0:T(8,128)(2,1)S(1)} collective-permute-done((bf16[1,256,128]{2,1,0:T(8,128)(2,1)S(1)}, bf16[1,256,128]{2,1,0:T(8,128)(2,1)S(1)}, u32[]{:S(2)}, u32[]{:S(2)}) %collective-permute-start.60) | collective-permute-done | bytes 65568 | tf_op jit(solution)/shard_map/ppermute | solution.py:221
  248.7 3.3 collective-permute-start.63
  256.7 4.6 collective-permute-done.64
  265.3 6.0 %fusion.212 = f32[1024,2048]{1,0:T(8,128)} fusion(bf16[2048,768]{1,0:T(8,128)(2,1)S(1)} %shard_map.487, bf16[1024,256]{0,1:T(8,128)(2,1)S(1)} %get-tuple-element.129, bf16[1024,256]{0,1:T(8,128)(2,1)S(1)} %fusion.82, bf16[1024,256]{0,1:T(8,128)(2,1)S(1)} %fusion.81), kind=kOutput, calls=%fused_computation.413 | convolution fusion | flops 3225944064 | bytes 13107200 | tf_op jit(solution)/shard_map/dot_general | solution.py:41
  271.4 11.1 %fusion.218 = (f32[2048]{0:T(1024)}, f32[2048]{0:T(1024)}, bf16[1024,2048]{1,0:T(8,128)(2,1)}, f32[2048]{0:T(1024)}, f32[2048]{0:T(1024)}) fusion(f32[1024]{0:T(1024)S(1)} %copy-done.72, f32[1024]{0:T(1024)S(1)} %copy-done.59, bf16[1024,2048]{1,0:T(8,128)(2,1)S(1)} %copy-done.11, f32[2048]{0:T(1024)S(1)} %bitcast.321, f32[1024,2048]{1,0:T(8,128)} %fusion.212, ...), kind=kOutput, calls=%fused_computation.415 | convolution fusion | flops 4322222080 | bytes 23126016 | tf_op jit(solution)/shard_map/dot_general | solution.py:41
  290.5 4.4 collective-permute-done.47
  295.6 3.4 collective-permute-done.48
  299.1 3.2 collective-permute-start.49
  302.3 7.0 %convolution_convert_fusion.2.field_ref = bf16[2048,768]{1,0:T(8,128)(2,1)S(1)} fusion(bf16[1024,256]{0,1:T(8,128)(2,1)} %copy-done.22, bf16[1024,256]{0,1:T(8,128)(2,1)S(1)} %fusion.82, bf16[1024,256]{0,1:T(8,128)(2,1)S(1)} %fusion.81, bf16[1024,2048]{1,0:T(8,128)(2,1)} %param.32, f32[2048]{0:T(1024)} %bitcast.315, f32[2048]{0:T(1024)} %bitcast.317, ...), kind=kOutput, calls=%fused_computation.60 | convolution fusion | flops 3240099840 | bytes 8937472 | tf_op jit(solution)/shard_map/dot_general | solution.py:35
  311.5 10.1 %shard_map.493 = bf16[16,128,768]{2,1,0:T(8,128)(2,1)S(1)} custom-call(s32[16]{0:T(128)S(1)} %get-tuple-element.166.place_ref, bf16[2048,768]{1,0:T(8,128)(2,1)S(1)} %convolution_convert_fusion.2.field_ref), custom_call_target="tpu_custom_call" | custom-call | tf_op jit(solution)/shard_map/pallas_call | solution.py:187
  324.8 3.0 collective-permute-start.38
  327.9 9.9 %collective-permute-done.51 = f32[80,128]{1,0:T(8,128)S(1)} collective-permute-done((f32[80,128]{1,0:T(8,128)S(1)}, f32[80,128]{1,0:T(8,128)S(1)}, u32[]{:S(2)}, u32[]{:S(2)}) %collective-permute-start.51) | collective-permute-done | bytes 40992 | tf_op jit(solution)/shard_map/ppermute | solution.py:275
  337.7 2.9 collective-permute-start.52
  350.5 2.8 collective-permute-start.39
  354.4 15.3 %collective-permute-done.28 = bf16[256,2048]{1,0:T(8,128)(2,1)} collective-permute-done((bf16[256,2048]{1,0:T(8,128)(2,1)}, bf16[256,2048]{1,0:T(8,128)(2,1)}, u32[]{:S(2)}, u32[]{:S(2)}) %collective-permute-start.28) | collective-permute-done | bytes 1048608 | tf_op jit(solution)/shard_map/ppermute | solution.py:244
  370.5 5.0 collective-permute-done.26
  385.0 5.6 %collective-permute-done.72 = bf16[1,1024,128]{2,1,0:T(8,128)(2,1)S(1)} collective-permute-done((bf16[1,1024,128]{2,1,0:T(8,128)(2,1)S(1)}, bf16[1,1024,128]{2,1,0:T(8,128)(2,1)S(1)}, u32[]{:S(2)}, u32[]{:S(2)}) %collective-permute-start.72) | collective-permute-done | bytes 262176 | tf_op jit(solution)/shard_map/ppermute | solution.py:221
  392.4 5.5 %collective-permute-done.68 = bf16[1,128,1024]{2,1,0:T(8,128)(2,1)S(1)} collective-permute-done((bf16[1,128,1024]{2,1,0:T(8,128)(2,1)S(1)}, bf16[1,128,1024]{2,1,0:T(8,128)(2,1)S(1)}, u32[]{:S(2)}, u32[]{:S(2)}) %collective-permute-start.68) | collective-permute-done | bytes 262176 | tf_op jit(solution)/shard_map/ppermute | solution.py:222
  399.3 6.1 %collective-permute-done.74 = bf16[1,1024,128]{2,1,0:T(8,128)(2,1)S(1)} collective-permute-done((bf16[1,1024,128]{2,1,0:T(8,128)(2,1)S(1)}, bf16[1,1024,128]{2,1,0:T(8,128)(2,1)S(1)}, u32[]{:S(2)}, u32[]{:S(2)}) %collective-permute-start.74) | collective-permute-done | bytes 262176 | tf_op jit(solution)/shard_map/ppermute | solution.py:222
  408.0 2.8 collective-permute-start.69
  412.0 15.7 %collective-permute-done.54 = bf16[1,128,768]{2,1,0:T(8,128)(2,1)S(1)} collective-permute-done((bf16[1,128,768]{2,1,0:T(8,128)(2,1)S(1)}, bf16[1,128,768]{2,1,0:T(8,128)(2,1)S(1)}, u32[]{:S(2)}, u32[]{:S(2)}) %collective-permute-start.54) | collective-permute-done | bytes 196640 | tf_op jit(solution)/shard_map/ppermute | solution.py:221
  432.8 4.6 collective-permute-done.75
  442.9 3.0 collective-permute-start.57
  452.5 4.5 fusion.52
  457.1 2.6 fusion.69
  466.6 4.7 fusion.16
  472.6 2.6 collective-permute-start.58
  475.5 3.2 collective-permute-start.31
  479.0 3.4 collective-permute-start.42
  486.5 16.2 %collective-permute-done.32.refs_4_ = bf16[2,128,2048]{2,1,0:T(8,128)(2,1)S(1)} collective-permute-done((bf16[2,128,2048]{2,1,0:T(8,128)(2,1)S(1)}, bf16[2,128,2048]{2,1,0:T(8,128)(2,1)S(1)}, u32[]{:S(2)}, u32[]{:S(2)}) %collective-permute-start.32) | collective-permute-done | bytes 1048608 | tf_op jit(solution)/shard_map/ppermute | solution.py:262
  502.9 3.3 collective-permute-start.34
  506.2 12.8 %collective-permute-done.43.refs_4_ = bf16[2,128,2048]{2,1,0:T(8,128)(2,1)S(1)} collective-permute-done((bf16[2,128,2048]{2,1,0:T(8,128)(2,1)S(1)}, bf16[2,128,2048]{2,1,0:T(8,128)(2,1)S(1)}, u32[]{:S(2)}, u32[]{:S(2)}) %collective-permute-start.43) | collective-permute-done | bytes 1048608 | tf_op jit(solution)/shard_map/ppermute | solution.py:262
  519.2 3.3 collective-permute-start.45
  526.5 3.0 shard_map.491
  530.3 3.0 shard_map.492
  (454 shorter events, 171.2 us)
Async XLA Ops:
  2.4 34.5 %collective-permute-start.7 = (bf16[1,256,128]{2,1,0:T(8,128)(2,1)}, bf16[1,256,128]{2,1,0:T(8,128)(2,1)S(1)}, u32[]{:S(2)}, u32[]{:S(2)}) collective-permute-start(bf16[1,256,128]{2,1,0:T(8,128)(2,1)} %get-tuple-element.88), channel_id=1, source_target_pairs={{0,8},{8,0},{1,9},{9,1},{2,10},{10,2},{3,11},{11,3},{4,12},{12,4},... | collective-permute-start | bytes 196616 | tf_op jit(solution)/shard_map/ppermute | solution.py:202
  8.1 42.7 %collective-permute-start = (bf16[1,128,768]{2,1,0:T(8,128)(2,1)}, bf16[1,128,768]{2,1,0:T(8,128)(2,1)}, u32[]{:S(2)}, u32[]{:S(2)}) collective-permute-start(bf16[1,128,768]{2,1,0:T(8,128)(2,1)} %get-tuple-element.90), channel_id=1, source_target_pairs={{0,8},{8,0},{1,9},{9,1},{2,10},{10,2},{3,11},{11,3},{4,12},{12,4},... | collective-permute-start | bytes 589832 | tf_op jit(solution)/shard_map/ppermute | solution.py:202
  10.0 43.5 %collective-permute-start.19 = (bf16[1,1024,128]{2,1,0:T(8,128)(2,1)}, bf16[1,1024,128]{2,1,0:T(8,128)(2,1)S(1)}, u32[]{:S(2)}, u32[]{:S(2)}) collective-permute-start(bf16[1,1024,128]{2,1,0:T(8,128)(2,1)} %get-tuple-element.92), channel_id=1, source_target_pairs={{0,8},{8,0},{1,9},{9,1},{2,10},{10,2},{3,11},{11,3},{4,12},{12,4},... | collective-permute-start | bytes 786440 | tf_op jit(solution)/shard_map/ppermute | solution.py:202
  15.4 49.1 %collective-permute-start.13 = (bf16[1,128,1024]{2,1,0:T(8,128)(2,1)}, bf16[1,128,1024]{2,1,0:T(8,128)(2,1)S(1)}, u32[]{:S(2)}, u32[]{:S(2)}) collective-permute-start(bf16[1,128,1024]{2,1,0:T(8,128)(2,1)} %get-tuple-element.96), channel_id=1, source_target_pairs={{0,8},{8,0},{1,9},{9,1},{2,10},{10,2},{3,11},{11,3},{4,12},{12,4},... | collective-permute-start | bytes 786440 | tf_op jit(solution)/shard_map/ppermute | solution.py:202
  45.8 12.0 %collective-permute-start.10 = (bf16[1,256,128]{2,1,0:T(8,128)(2,1)S(1)}, bf16[1,256,128]{2,1,0:T(8,128)(2,1)S(1)}, u32[]{:S(2)}, u32[]{:S(2)}) collective-permute-start(bf16[1,256,128]{2,1,0:T(8,128)(2,1)S(1)} %slice.489), channel_id=1, source_target_pairs={{0,32},{32,64},{64,96},{96,0},{1,33},{33,65},{65,97},{97,1},{2,34}... | collective-permute-start | bytes 196616 | tf_op jit(solution)/shard_map/ppermute | solution.py:205
  47.0 10.9 %collective-permute-start.11 = (bf16[1,256,128]{2,1,0:T(8,128)(2,1)S(1)}, bf16[1,256,128]{2,1,0:T(8,128)(2,1)S(1)}, u32[]{:S(2)}, u32[]{:S(2)}) collective-permute-start(bf16[1,256,128]{2,1,0:T(8,128)(2,1)S(1)} %slice.490), channel_id=1, source_target_pairs={{0,96},{32,0},{64,32},{96,64},{1,97},{33,1},{65,33},{97,65},{2,98}... | collective-permute-start | bytes 196616 | tf_op jit(solution)/shard_map/ppermute | solution.py:206
  51.9 12.6 %collective-permute-start.2 = (bf16[2,128,768]{2,1,0:T(8,128)(2,1)S(1)}, bf16[2,128,768]{2,1,0:T(8,128)(2,1)S(1)}, u32[]{:S(2)}, u32[]{:S(2)}) collective-permute-start(bf16[2,128,768]{2,1,0:T(8,128)(2,1)S(1)} %pad_maximum_fusion.21), channel_id=1, source_target_pairs={{0,32},{32,64},{64,96},{96,0},{1,33},{33,65},{65,97},{97,1},{2,34}... | collective-permute-start | bytes 1179656 | tf_op jit(solution)/shard_map/ppermute | solution.py:203
  53.5 12.8 %collective-permute-start.1 = (bf16[2,128,768]{2,1,0:T(8,128)(2,1)S(1)}, bf16[2,128,768]{2,1,0:T(8,128)(2,1)S(1)}, u32[]{:S(2)}, u32[]{:S(2)}) collective-permute-start(bf16[2,128,768]{2,1,0:T(8,128)(2,1)S(1)} %pad_maximum_fusion.21), channel_id=1, source_target_pairs={{0,96},{32,0},{64,32},{96,64},{1,97},{33,1},{65,33},{97,65},{2,98}... | collective-permute-start | bytes 1179656 | tf_op jit(solution)/shard_map/ppermute | solution.py:204
  57.8 21.5 %collective-permute-start.21 = (bf16[2,1024,128]{2,1,0:T(8,128)(2,1)S(1)}, bf16[2,1024,128]{2,1,0:T(8,128)(2,1)S(1)}, u32[]{:S(2)}, u32[]{:S(2)}) collective-permute-start(bf16[2,1024,128]{2,1,0:T(8,128)(2,1)S(1)} %pad_maximum_fusion.16), channel_id=1, source_target_pairs={{0,32},{32,64},{64,96},{96,0},{1,33},{33,65},{65,97},{97,1},{2,34}... | collective-permute-start | bytes 1572872 | tf_op jit(solution)/shard_map/ppermute | solution.py:203
  57.9 30.2 %collective-permute-start.20 = (bf16[2,1024,128]{2,1,0:T(8,128)(2,1)S(1)}, bf16[2,1024,128]{2,1,0:T(8,128)(2,1)S(1)}, u32[]{:S(2)}, u32[]{:S(2)}) collective-permute-start(bf16[2,1024,128]{2,1,0:T(8,128)(2,1)S(1)} %pad_maximum_fusion.16), channel_id=1, source_target_pairs={{0,96},{32,0},{64,32},{96,64},{1,97},{33,1},{65,33},{97,65},{2,98}... | collective-permute-start | bytes 1572872 | tf_op jit(solution)/shard_map/ppermute | solution.py:204
  64.5 18.7 %collective-permute-start.12 = (bf16[8,256,128]{2,1,0:T(8,128)(2,1)S(1)}, bf16[8,256,128]{2,1,0:T(8,128)(2,1)S(1)}, u32[]{:S(2)}, u32[]{:S(2)}) collective-permute-start(bf16[8,256,128]{2,1,0:T(8,128)(2,1)S(1)} %constant_dynamic-update-slice_fusion.6.refs_0_), channel_id=1, source_target_pairs={{0,16},{16,0},{1,17},{17,1},{2,18},{18,2},{3,19},{19,3},{4,20},{20... | collective-permute-start | bytes 1572872 | tf_op jit(solution)/shard_map/ppermute | solution.py:208
  64.5 12.4 %collective-permute-start.3 = (bf16[1,128,768]{2,1,0:T(8,128)(2,1)S(1)}, bf16[1,128,768]{2,1,0:T(8,128)(2,1)S(1)}, u32[]{:S(2)}, u32[]{:S(2)}) collective-permute-start(bf16[1,128,768]{2,1,0:T(8,128)(2,1)S(1)} %slice.476), channel_id=1, source_target_pairs={{0,32},{32,64},{64,96},{96,0},{1,33},{33,65},{65,97},{97,1},{2,34}... | collective-permute-start | bytes 589832 | tf_op jit(solution)/shard_map/ppermute | solution.py:205
  66.4 11.5 %collective-permute-start.4 = (bf16[1,128,768]{2,1,0:T(8,128)(2,1)S(1)}, bf16[1,128,768]{2,1,0:T(8,128)(2,1)S(1)}, u32[]{:S(2)}, u32[]{:S(2)}) collective-permute-start(bf16[1,128,768]{2,1,0:T(8,128)(2,1)S(1)} %slice.477), channel_id=1, source_target_pairs={{0,96},{32,0},{64,32},{96,64},{1,97},{33,1},{65,33},{97,65},{2,98}... | collective-permute-start | bytes 589832 | tf_op jit(solution)/shard_map/ppermute | solution.py:206
  77.0 14.5 %collective-permute-start.15 = (bf16[2,128,1024]{2,1,0:T(8,128)(2,1)S(1)}, bf16[2,128,1024]{2,1,0:T(8,128)(2,1)S(1)}, u32[]{:S(2)}, u32[]{:S(2)}) collective-permute-start(bf16[2,128,1024]{2,1,0:T(8,128)(2,1)S(1)} %pad_maximum_fusion.15), channel_id=1, source_target_pairs={{0,32},{32,64},{64,96},{96,0},{1,33},{33,65},{65,97},{97,1},{2,34}... | collective-permute-start | bytes 1572872 | tf_op jit(solution)/shard_map/ppermute | solution.py:203
  79.3 27.1 %collective-permute-start.5 = (bf16[8,128,768]{2,1,0:T(8,128)(2,1)}, bf16[8,128,768]{2,1,0:T(8,128)(2,1)S(1)}, u32[]{:S(2)}, u32[]{:S(2)}) collective-permute-start(bf16[8,128,768]{2,1,0:T(8,128)(2,1)} %constant_dynamic-update-slice_fusion.refs_0_), channel_id=1, source_target_pairs={{0,16},{16,0},{1,17},{17,1},{2,18},{18,2},{3,19},{19,3},{4,20},{20... | collective-permute-start | bytes 4718600 | tf_op jit(solution)/shard_map/ppermute | solution.py:208
  79.4 16.0 %collective-permute-start.14 = (bf16[2,128,1024]{2,1,0:T(8,128)(2,1)S(1)}, bf16[2,128,1024]{2,1,0:T(8,128)(2,1)S(1)}, u32[]{:S(2)}, u32[]{:S(2)}) collective-permute-start(bf16[2,128,1024]{2,1,0:T(8,128)(2,1)S(1)} %pad_maximum_fusion.15), channel_id=1, source_target_pairs={{0,96},{32,0},{64,32},{96,64},{1,97},{33,1},{65,33},{97,65},{2,98}... | collective-permute-start | bytes 1572872 | tf_op jit(solution)/shard_map/ppermute | solution.py:204
  83.2 16.1 %collective-permute-start.22 = (bf16[1,1024,128]{2,1,0:T(8,128)(2,1)S(1)}, bf16[1,1024,128]{2,1,0:T(8,128)(2,1)S(1)}, u32[]{:S(2)}, u32[]{:S(2)}) collective-permute-start(bf16[1,1024,128]{2,1,0:T(8,128)(2,1)S(1)} %slice.493), channel_id=1, source_target_pairs={{0,32},{32,64},{64,96},{96,0},{1,33},{33,65},{65,97},{97,1},{2,34}... | collective-permute-start | bytes 786440 | tf_op jit(solution)/shard_map/ppermute | solution.py:205
  88.2 12.8 %collective-permute-start.23 = (bf16[1,1024,128]{2,1,0:T(8,128)(2,1)S(1)}, bf16[1,1024,128]{2,1,0:T(8,128)(2,1)S(1)}, u32[]{:S(2)}, u32[]{:S(2)}) collective-permute-start(bf16[1,1024,128]{2,1,0:T(8,128)(2,1)S(1)} %slice.494), channel_id=1, source_target_pairs={{0,96},{32,0},{64,32},{96,64},{1,97},{33,1},{65,33},{97,65},{2,98}... | collective-permute-start | bytes 786440 | tf_op jit(solution)/shard_map/ppermute | solution.py:206
  91.5 9.7 %collective-permute-start.16 = (bf16[1,128,1024]{2,1,0:T(8,128)(2,1)S(1)}, bf16[1,128,1024]{2,1,0:T(8,128)(2,1)S(1)}, u32[]{:S(2)}, u32[]{:S(2)}) collective-permute-start(bf16[1,128,1024]{2,1,0:T(8,128)(2,1)S(1)} %slice.491), channel_id=1, source_target_pairs={{0,32},{32,64},{64,96},{96,0},{1,33},{33,65},{65,97},{97,1},{2,34}... | collective-permute-start | bytes 786440 | tf_op jit(solution)/shard_map/ppermute | solution.py:205
  95.4 10.8 %collective-permute-start.17 = (bf16[1,128,1024]{2,1,0:T(8,128)(2,1)S(1)}, bf16[1,128,1024]{2,1,0:T(8,128)(2,1)S(1)}, u32[]{:S(2)}, u32[]{:S(2)}) collective-permute-start(bf16[1,128,1024]{2,1,0:T(8,128)(2,1)S(1)} %slice.492), channel_id=1, source_target_pairs={{0,96},{32,0},{64,32},{96,64},{1,97},{33,1},{65,33},{97,65},{2,98}... | collective-permute-start | bytes 786440 | tf_op jit(solution)/shard_map/ppermute | solution.py:206
  101.1 44.5 %collective-permute-start.24 = (bf16[8,1024,128]{2,1,0:T(8,128)(2,1)S(1)}, bf16[8,1024,128]{2,1,0:T(8,128)(2,1)S(1)}, u32[]{:S(2)}, u32[]{:S(2)}) collective-permute-start(bf16[8,1024,128]{2,1,0:T(8,128)(2,1)S(1)} %constant_dynamic-update-slice_fusion.18.refs_0_), channel_id=1, source_target_pairs={{0,16},{16,0},{1,17},{17,1},{2,18},{18,2},{3,19},{19,3},{4,20},{20... | collective-permute-start | bytes 6291464 | tf_op jit(solution)/shard_map/ppermute | solution.py:208
  106.3 22.0 %collective-permute-start.18 = (bf16[8,128,1024]{2,1,0:T(8,128)(2,1)S(1)}, bf16[8,128,1024]{2,1,0:T(8,128)(2,1)S(1)}, u32[]{:S(2)}, u32[]{:S(2)}) collective-permute-start(bf16[8,128,1024]{2,1,0:T(8,128)(2,1)S(1)} %constant_dynamic-update-slice_fusion.12.refs_0_), channel_id=1, source_target_pairs={{0,16},{16,0},{1,17},{17,1},{2,18},{18,2},{3,19},{19,3},{4,20},{20... | collective-permute-start | bytes 6291464 | tf_op jit(solution)/shard_map/ppermute | solution.py:208
  122.5 63.3 %collective-permute-start.6 = (bf16[2,1024,256]{1,2,0:T(8,128)(2,1)}, bf16[2,1024,256]{1,2,0:T(8,128)(2,1)S(1)}, u32[]{:S(2)}, u32[]{:S(2)}) collective-permute-start(bf16[2,1024,256]{1,2,0:T(8,128)(2,1)} %pad_maximum_fusion.1), channel_id=1, source_target_pairs={{0,8},{1,9},{2,10},{3,11},{4,12},{5,13},{6,14},{7,15},{16,24},{17,... | collective-permute-start | bytes 3145736 | tf_op jit(solution)/shard_map/ppermute | solution.py:353
  166.9 183.6 %collective-permute-start.65 = (bf16[8,128,1024]{2,1,0:T(8,128)(2,1)}, bf16[8,128,1024]{2,1,0:T(8,128)(2,1)}, u32[]{:S(2)}, u32[]{:S(2)}) collective-permute-start(bf16[8,128,1024]{2,1,0:T(8,128)(2,1)} %slice.543), channel_id=1, source_target_pairs={{0,16},{16,0},{1,17},{17,1},{2,18},{18,2},{3,19},{19,3},{4,20},{20... | collective-permute-start | bytes 6291464 | tf_op jit(solution)/shard_map/ppermute | solution.py:216
  178.9 199.7 %collective-permute-start.71 = (bf16[8,1024,128]{2,1,0:T(8,128)(2,1)}, bf16[8,1024,128]{2,1,0:T(8,128)(2,1)}, u32[]{:S(2)}, u32[]{:S(2)}) collective-permute-start(bf16[8,1024,128]{2,1,0:T(8,128)(2,1)} %slice.560), channel_id=1, source_target_pairs={{0,16},{16,0},{1,17},{17,1},{2,18},{18,2},{3,19},{19,3},{4,20},{20... | collective-permute-start | bytes 6291464 | tf_op jit(solution)/shard_map/ppermute | solution.py:216
  221.2 15.3 %collective-permute-start.25 = (bf16[128,2048]{1,0:T(8,128)(2,1)S(1)}, bf16[128,2048]{1,0:T(8,128)(2,1)S(1)}, u32[]{:S(2)}, u32[]{:S(2)}) collective-permute-start(bf16[128,2048]{1,0:T(8,128)(2,1)S(1)} %get-tuple-element.122), channel_id=1, source_target_pairs={{0,2},{2,4},{4,6},{6,0},{1,3},{3,5},{5,7},{7,1},{8,10},{10,12},{12... | collective-permute-start | bytes 1572872 | tf_op jit(solution)/shard_map/ppermute | solution.py:239
  222.7 13.7 %collective-permute-start.27 = (bf16[128,2048]{1,0:T(8,128)(2,1)S(1)}, bf16[128,2048]{1,0:T(8,128)(2,1)S(1)}, u32[]{:S(2)}, u32[]{:S(2)}) collective-permute-start(bf16[128,2048]{1,0:T(8,128)(2,1)S(1)} %get-tuple-element.123), channel_id=1, source_target_pairs={{0,6},{2,0},{4,2},{6,4},{1,7},{3,1},{5,3},{7,5},{8,14},{10,8},{12,... | collective-permute-start | bytes 1572872 | tf_op jit(solution)/shard_map/ppermute | solution.py:240
  224.7 38.2 %collective-permute-start.35 = (bf16[2,1024,256]{1,2,0:T(8,128)(2,1)S(1)}, bf16[2,1024,256]{1,2,0:T(8,128)(2,1)S(1)}, u32[]{:S(2)}, u32[]{:S(2)}) collective-permute-start(bf16[2,1024,256]{1,2,0:T(8,128)(2,1)S(1)} %pad_maximum_fusion.7), channel_id=1, source_target_pairs={{8,0},{9,1},{10,2},{11,3},{12,4},{13,5},{14,6},{15,7},{24,16},{25,... | collective-permute-start | bytes 3145736 | tf_op jit(solution)/shard_map/ppermute | solution.py:374
  299.1 10.2 %collective-permute-start.49 = (f32[94,128]{1,0:T(8,128)S(1)}, f32[94,128]{1,0:T(8,128)S(1)}, u32[]{:S(2)}, u32[]{:S(2)}) collective-permute-start(f32[94,128]{1,0:T(8,128)S(1)} %add.734), channel_id=1, source_target_pairs={{0,64},{32,96},{64,0},{96,32},{1,65},{33,97},{65,1},{97,33},{2,66}... | collective-permute-start | bytes 144392 | tf_op jit(solution)/shard_map/ppermute | solution.py:275
  309.3 18.5 %collective-permute-start.50 = (f32[80,128]{1,0:T(8,128)S(1)}, f32[80,128]{1,0:T(8,128)S(1)}, u32[]{:S(2)}, u32[]{:S(2)}) collective-permute-start(f32[80,128]{1,0:T(8,128)S(1)} %slice.505), channel_id=1, source_target_pairs={{0,1},{1,0},{2,3},{3,2},{4,5},{5,4},{6,7},{7,6},{8,9},{9,8},{10,11... | collective-permute-start | bytes 122888 | tf_op jit(solution)/shard_map/ppermute | solution.py:275
  324.5 23.4 %collective-permute-start.36 = (bf16[128,2048]{1,0:T(8,128)(2,1)}, bf16[128,2048]{1,0:T(8,128)(2,1)}, u32[]{:S(2)}, u32[]{:S(2)}) collective-permute-start(bf16[128,2048]{1,0:T(8,128)(2,1)} %get-tuple-element.116), channel_id=1, source_target_pairs={{0,2},{2,4},{4,6},{6,0},{1,3},{3,5},{5,7},{7,1},{8,10},{10,12},{12... | collective-permute-start | bytes 1572872 | tf_op jit(solution)/shard_map/ppermute | solution.py:239
  324.8 23.6 %collective-permute-start.38 = (bf16[128,2048]{1,0:T(8,128)(2,1)}, bf16[128,2048]{1,0:T(8,128)(2,1)}, u32[]{:S(2)}, u32[]{:S(2)}) collective-permute-start(bf16[128,2048]{1,0:T(8,128)(2,1)} %get-tuple-element.117), channel_id=1, source_target_pairs={{0,6},{2,0},{4,2},{6,4},{1,7},{3,1},{5,3},{7,5},{8,14},{10,8},{12,... | collective-permute-start | bytes 1572872 | tf_op jit(solution)/shard_map/ppermute | solution.py:240
  327.8 10.0 %collective-permute-start.51 = (f32[80,128]{1,0:T(8,128)S(1)}, f32[80,128]{1,0:T(8,128)S(1)}, u32[]{:S(2)}, u32[]{:S(2)}) collective-permute-start(f32[80,128]{1,0:T(8,128)S(1)} %slice_add_fusion.4), channel_id=1, source_target_pairs={{0,2},{2,0},{4,6},{6,4},{1,3},{3,1},{5,7},{7,5},{8,10},{10,8},{12,... | collective-permute-start | bytes 122888 | tf_op jit(solution)/shard_map/ppermute | solution.py:275
  343.2 26.4 %collective-permute-start.28 = (bf16[256,2048]{1,0:T(8,128)(2,1)}, bf16[256,2048]{1,0:T(8,128)(2,1)}, u32[]{:S(2)}, u32[]{:S(2)}) collective-permute-start(bf16[256,2048]{1,0:T(8,128)(2,1)} %pad_maximum_fusion.5), channel_id=1, source_target_pairs={{0,6},{2,0},{4,2},{6,4},{1,7},{3,1},{5,3},{7,5},{8,14},{10,8},{12,... | collective-permute-start | bytes 3145736 | tf_op jit(solution)/shard_map/ppermute | solution.py:244
  347.9 27.5 %collective-permute-start.26 = (bf16[256,2048]{1,0:T(8,128)(2,1)}, bf16[256,2048]{1,0:T(8,128)(2,1)S(1)}, u32[]{:S(2)}, u32[]{:S(2)}) collective-permute-start(bf16[256,2048]{1,0:T(8,128)(2,1)} %pad_maximum_fusion.4), channel_id=1, source_target_pairs={{0,2},{2,4},{4,6},{6,0},{1,3},{3,5},{5,7},{7,1},{8,10},{10,12},{12... | collective-permute-start | bytes 3145736 | tf_op jit(solution)/shard_map/ppermute | solution.py:243
  348.4 58.9 %collective-permute-start.53 = (bf16[8,128,768]{2,1,0:T(8,128)(2,1)}, bf16[8,128,768]{2,1,0:T(8,128)(2,1)S(1)}, u32[]{:S(2)}, u32[]{:S(2)}) collective-permute-start(bf16[8,128,768]{2,1,0:T(8,128)(2,1)} %slice.509), channel_id=1, source_target_pairs={{0,16},{16,0},{1,17},{17,1},{2,18},{18,2},{3,19},{19,3},{4,20},{20... | collective-permute-start | bytes 4718600 | tf_op jit(solution)/shard_map/ppermute | solution.py:216
  350.5 57.5 %collective-permute-start.39 = (bf16[256,2048]{1,0:T(8,128)(2,1)S(1)}, bf16[256,2048]{1,0:T(8,128)(2,1)S(1)}, u32[]{:S(2)}, u32[]{:S(2)}) collective-permute-start(bf16[256,2048]{1,0:T(8,128)(2,1)S(1)} %pad_maximum_fusion.9), channel_id=1, source_target_pairs={{0,6},{2,0},{4,2},{6,4},{1,7},{3,1},{5,3},{7,5},{8,14},{10,8},{12,... | collective-permute-start | bytes 3145736 | tf_op jit(solution)/shard_map/ppermute | solution.py:244
  369.7 41.1 %collective-permute-start.37 = (bf16[256,2048]{1,0:T(8,128)(2,1)S(1)}, bf16[256,2048]{1,0:T(8,128)(2,1)S(1)}, u32[]{:S(2)}, u32[]{:S(2)}) collective-permute-start(bf16[256,2048]{1,0:T(8,128)(2,1)S(1)} %pad_maximum_fusion.8), channel_id=1, source_target_pairs={{0,2},{2,4},{4,6},{6,0},{1,3},{3,5},{5,7},{7,1},{8,10},{10,12},{12... | collective-permute-start | bytes 3145736 | tf_op jit(solution)/shard_map/ppermute | solution.py:243
  375.4 7.6 %collective-permute-start.66 = (bf16[1,128,1024]{2,1,0:T(8,128)(2,1)S(1)}, bf16[1,128,1024]{2,1,0:T(8,128)(2,1)S(1)}, u32[]{:S(2)}, u32[]{:S(2)}) collective-permute-start(bf16[1,128,1024]{2,1,0:T(8,128)(2,1)S(1)} %add_convert_fusion.21), channel_id=1, source_target_pairs={{0,32},{32,64},{64,96},{96,0},{1,33},{33,65},{65,97},{97,1},{2,34}... | collective-permute-start | bytes 786440 | tf_op jit(solution)/shard_map/ppermute | solution.py:221
  378.5 78.5 %collective-permute-start.29 = (bf16[128,2048]{1,0:T(8,128)(2,1)S(1)}, bf16[128,2048]{1,0:T(8,128)(2,1)S(1)}, u32[]{:S(2)}, u32[]{:S(2)}) collective-permute-start(bf16[128,2048]{1,0:T(8,128)(2,1)S(1)} %add_convert_fusion.7), channel_id=1, source_target_pairs={{0,1},{1,0},{2,3},{3,2},{4,5},{5,4},{6,7},{7,6},{8,9},{9,8},{10,11... | collective-permute-start | bytes 1572872 | tf_op jit(solution)/shard_map/ppermute | solution.py:252
  383.0 7.6 %collective-permute-start.72 = (bf16[1,1024,128]{2,1,0:T(8,128)(2,1)S(1)}, bf16[1,1024,128]{2,1,0:T(8,128)(2,1)S(1)}, u32[]{:S(2)}, u32[]{:S(2)}) collective-permute-start(bf16[1,1024,128]{2,1,0:T(8,128)(2,1)S(1)} %add_convert_fusion.15), channel_id=1, source_target_pairs={{0,32},{32,64},{64,96},{96,0},{1,33},{33,65},{65,97},{97,1},{2,34}... | collective-permute-start | bytes 786440 | tf_op jit(solution)/shard_map/ppermute | solution.py:221
  397.9 7.5 %collective-permute-start.74 = (bf16[1,1024,128]{2,1,0:T(8,128)(2,1)S(1)}, bf16[1,1024,128]{2,1,0:T(8,128)(2,1)S(1)}, u32[]{:S(2)}, u32[]{:S(2)}) collective-permute-start(bf16[1,1024,128]{2,1,0:T(8,128)(2,1)S(1)} %get-tuple-element.101), channel_id=1, source_target_pairs={{0,96},{32,0},{64,32},{96,64},{1,97},{33,1},{65,33},{97,65},{2,98}... | collective-permute-start | bytes 786440 | tf_op jit(solution)/shard_map/ppermute | solution.py:222
  405.4 22.8 %collective-permute-start.67 = (bf16[2,128,1024]{2,1,0:T(8,128)(2,1)S(1)}, bf16[2,128,1024]{2,1,0:T(8,128)(2,1)S(1)}, u32[]{:S(2)}, u32[]{:S(2)}) collective-permute-start(bf16[2,128,1024]{2,1,0:T(8,128)(2,1)S(1)} %pad_maximum_fusion.17), channel_id=1, source_target_pairs={{0,32},{32,64},{64,96},{96,0},{1,33},{33,65},{65,97},{97,1},{2,34}... | collective-permute-start | bytes 1572872 | tf_op jit(solution)/shard_map/ppermute | solution.py:225
  407.3 23.9 %collective-permute-start.73 = (bf16[2,1024,128]{2,1,0:T(8,128)(2,1)S(1)}, bf16[2,1024,128]{2,1,0:T(8,128)(2,1)S(1)}, u32[]{:S(2)}, u32[]{:S(2)}) collective-permute-start(bf16[2,1024,128]{2,1,0:T(8,128)(2,1)S(1)} %pad_maximum_fusion.19), channel_id=1, source_target_pairs={{0,32},{32,64},{64,96},{96,0},{1,33},{33,65},{65,97},{97,1},{2,34}... | collective-permute-start | bytes 1572872 | tf_op jit(solution)/shard_map/ppermute | solution.py:225
  408.0 21.3 %collective-permute-start.69 = (bf16[2,128,1024]{2,1,0:T(8,128)(2,1)S(1)}, bf16[2,128,1024]{2,1,0:T(8,128)(2,1)S(1)}, u32[]{:S(2)}, u32[]{:S(2)}) collective-permute-start(bf16[2,128,1024]{2,1,0:T(8,128)(2,1)S(1)} %pad_maximum_fusion.18), channel_id=1, source_target_pairs={{0,96},{32,0},{64,32},{96,64},{1,97},{33,1},{65,33},{97,65},{2,98}... | collective-permute-start | bytes 1572872 | tf_op jit(solution)/shard_map/ppermute | solution.py:226
  410.8 17.0 %collective-permute-start.54 = (bf16[1,128,768]{2,1,0:T(8,128)(2,1)S(1)}, bf16[1,128,768]{2,1,0:T(8,128)(2,1)S(1)}, u32[]{:S(2)}, u32[]{:S(2)}) collective-permute-start(bf16[1,128,768]{2,1,0:T(8,128)(2,1)S(1)} %add_convert_fusion.27), channel_id=1, source_target_pairs={{0,32},{32,64},{64,96},{96,0},{1,33},{33,65},{65,97},{97,1},{2,34}... | collective-permute-start | bytes 589832 | tf_op jit(solution)/shard_map/ppermute | solution.py:221
  427.7 9.7 %collective-permute-start.75 = (bf16[2,1024,128]{2,1,0:T(8,128)(2,1)S(1)}, bf16[2,1024,128]{2,1,0:T(8,128)(2,1)S(1)}, u32[]{:S(2)}, u32[]{:S(2)}) collective-permute-start(bf16[2,1024,128]{2,1,0:T(8,128)(2,1)S(1)} %pad_maximum_fusion.20), channel_id=1, source_target_pairs={{0,96},{32,0},{64,32},{96,64},{1,97},{33,1},{65,33},{97,65},{2,98}... | collective-permute-start | bytes 1572872 | tf_op jit(solution)/shard_map/ppermute | solution.py:226
  428.2 14.7 %collective-permute-start.40 = (bf16[128,2048]{1,0:T(8,128)(2,1)S(1)}, bf16[128,2048]{1,0:T(8,128)(2,1)S(1)}, u32[]{:S(2)}, u32[]{:S(2)}) collective-permute-start(bf16[128,2048]{1,0:T(8,128)(2,1)S(1)} %add_convert_fusion.2), channel_id=1, source_target_pairs={{0,1},{1,0},{2,3},{3,2},{4,5},{5,4},{6,7},{7,6},{8,9},{9,8},{10,11... | collective-permute-start | bytes 1572872 | tf_op jit(solution)/shard_map/ppermute | solution.py:252
  429.3 11.6 %collective-permute-start.56 = (bf16[1,128,768]{2,1,0:T(8,128)(2,1)S(1)}, bf16[1,128,768]{2,1,0:T(8,128)(2,1)S(1)}, u32[]{:S(2)}, u32[]{:S(2)}) collective-permute-start(bf16[1,128,768]{2,1,0:T(8,128)(2,1)S(1)} %get-tuple-element.109), channel_id=1, source_target_pairs={{0,96},{32,0},{64,32},{96,64},{1,97},{33,1},{65,33},{97,65},{2,98}... | collective-permute-start | bytes 589832 | tf_op jit(solution)/shard_map/ppermute | solution.py:222
  431.2 41.1 %collective-permute-start.55 = (bf16[2,128,768]{2,1,0:T(8,128)(2,1)S(1)}, bf16[2,128,768]{2,1,0:T(8,128)(2,1)S(1)}, u32[]{:S(2)}, u32[]{:S(2)}) collective-permute-start(bf16[2,128,768]{2,1,0:T(8,128)(2,1)S(1)} %pad_maximum_fusion.22), channel_id=1, source_target_pairs={{0,32},{32,64},{64,96},{96,0},{1,33},{33,65},{65,97},{97,1},{2,34}... | collective-permute-start | bytes 1179656 | tf_op jit(solution)/shard_map/ppermute | solution.py:225
  437.4 10.3 %collective-permute-start.70 = (bf16[1,128,1024]{2,1,0:T(8,128)(2,1)S(1)}, bf16[1,128,1024]{2,1,0:T(8,128)(2,1)S(1)}, u32[]{:S(2)}, u32[]{:S(2)}) collective-permute-start(bf16[1,128,1024]{2,1,0:T(8,128)(2,1)S(1)} %slice.694), channel_id=1, source_target_pairs={{0,8},{8,0},{1,9},{9,1},{2,10},{10,2},{3,11},{11,3},{4,12},{12,4},... | collective-permute-start | bytes 786440 | tf_op jit(solution)/shard_map/ppermute | solution.py:228
  440.9 22.2 %collective-permute-start.76 = (bf16[1,1024,128]{2,1,0:T(8,128)(2,1)S(1)}, bf16[1,1024,128]{2,1,0:T(8,128)(2,1)S(1)}, u32[]{:S(2)}, u32[]{:S(2)}) collective-permute-start(bf16[1,1024,128]{2,1,0:T(8,128)(2,1)S(1)} %slice.693), channel_id=1, source_target_pairs={{0,8},{8,0},{1,9},{9,1},{2,10},{10,2},{3,11},{11,3},{4,12},{12,4},... | collective-permute-start | bytes 786440 | tf_op jit(solution)/shard_map/ppermute | solution.py:228
  442.9 29.4 %collective-permute-start.57 = (bf16[2,128,768]{2,1,0:T(8,128)(2,1)S(1)}, bf16[2,128,768]{2,1,0:T(8,128)(2,1)S(1)}, u32[]{:S(2)}, u32[]{:S(2)}) collective-permute-start(bf16[2,128,768]{2,1,0:T(8,128)(2,1)S(1)} %pad_maximum_fusion.23), channel_id=1, source_target_pairs={{0,96},{32,0},{64,32},{96,64},{1,97},{33,1},{65,33},{97,65},{2,98}... | collective-permute-start | bytes 1179656 | tf_op jit(solution)/shard_map/ppermute | solution.py:226
  459.7 19.0 %collective-permute-start.41 = (bf16[128,2048]{1,0:T(8,128)(2,1)S(1)}, bf16[128,2048]{1,0:T(8,128)(2,1)S(1)}, u32[]{:S(2)}, u32[]{:S(2)}) collective-permute-start(bf16[128,2048]{1,0:T(8,128)(2,1)S(1)} %get-tuple-element.112), channel_id=1, source_target_pairs={{0,1},{1,0},{2,3},{3,2},{4,5},{5,4},{6,7},{7,6},{8,9},{9,8},{10,11... | collective-permute-start | bytes 1572872 | tf_op jit(solution)/shard_map/ppermute | solution.py:258
  460.2 15.0 %collective-permute-start.30 = (bf16[128,2048]{1,0:T(8,128)(2,1)S(1)}, bf16[128,2048]{1,0:T(8,128)(2,1)S(1)}, u32[]{:S(2)}, u32[]{:S(2)}) collective-permute-start(bf16[128,2048]{1,0:T(8,128)(2,1)S(1)} %get-tuple-element.113), channel_id=1, source_target_pairs={{0,1},{1,0},{2,3},{3,2},{4,5},{5,4},{6,7},{7,6},{8,9},{9,8},{10,11... | collective-permute-start | bytes 1572872 | tf_op jit(solution)/shard_map/ppermute | solution.py:258
  472.6 10.5 %collective-permute-start.58 = (bf16[1,128,768]{2,1,0:T(8,128)(2,1)S(1)}, bf16[1,128,768]{2,1,0:T(8,128)(2,1)S(1)}, u32[]{:S(2)}, u32[]{:S(2)}) collective-permute-start(bf16[1,128,768]{2,1,0:T(8,128)(2,1)S(1)} %slice.695), channel_id=1, source_target_pairs={{0,8},{8,0},{1,9},{9,1},{2,10},{10,2},{3,11},{11,3},{4,12},{12,4},... | collective-permute-start | bytes 589832 | tf_op jit(solution)/shard_map/ppermute | solution.py:228
  475.4 27.4 %collective-permute-start.32 = (bf16[2,128,2048]{2,1,0:T(8,128)(2,1)S(1)}, bf16[2,128,2048]{2,1,0:T(8,128)(2,1)S(1)}, u32[]{:S(2)}, u32[]{:S(2)}) collective-permute-start(bf16[2,128,2048]{2,1,0:T(8,128)(2,1)S(1)} %pad_maximum_fusion.6.refs_0_), channel_id=1, source_target_pairs={{0,2},{2,4},{4,6},{6,0},{1,3},{3,5},{5,7},{7,1},{8,10},{10,12},{12... | collective-permute-start | bytes 3145736 | tf_op jit(solution)/shard_map/ppermute | solution.py:262
  475.5 27.4 %collective-permute-start.31 = (bf16[2,128,2048]{2,1,0:T(8,128)(2,1)S(1)}, bf16[2,128,2048]{2,1,0:T(8,128)(2,1)S(1)}, u32[]{:S(2)}, u32[]{:S(2)}) collective-permute-start(bf16[2,128,2048]{2,1,0:T(8,128)(2,1)S(1)} %pad_maximum_fusion.6.refs_0_), channel_id=1, source_target_pairs={{0,6},{2,0},{4,2},{6,4},{1,7},{3,1},{5,3},{7,5},{8,14},{10,8},{12,... | collective-permute-start | bytes 3145736 | tf_op jit(solution)/shard_map/ppermute | solution.py:263
  478.9 40.2 %collective-permute-start.43 = (bf16[2,128,2048]{2,1,0:T(8,128)(2,1)S(1)}, bf16[2,128,2048]{2,1,0:T(8,128)(2,1)S(1)}, u32[]{:S(2)}, u32[]{:S(2)}) collective-permute-start(bf16[2,128,2048]{2,1,0:T(8,128)(2,1)S(1)} %pad_maximum_fusion.10.refs_0_), channel_id=1, source_target_pairs={{0,2},{2,4},{4,6},{6,0},{1,3},{3,5},{5,7},{7,1},{8,10},{10,12},{12... | collective-permute-start | bytes 3145736 | tf_op jit(solution)/shard_map/ppermute | solution.py:262
  479.0 40.2 %collective-permute-start.42 = (bf16[2,128,2048]{2,1,0:T(8,128)(2,1)S(1)}, bf16[2,128,2048]{2,1,0:T(8,128)(2,1)S(1)}, u32[]{:S(2)}, u32[]{:S(2)}) collective-permute-start(bf16[2,128,2048]{2,1,0:T(8,128)(2,1)S(1)} %pad_maximum_fusion.10.refs_0_), channel_id=1, source_target_pairs={{0,6},{2,0},{4,2},{6,4},{1,7},{3,1},{5,3},{7,5},{8,14},{10,8},{12,... | collective-permute-start | bytes 3145736 | tf_op jit(solution)/shard_map/ppermute | solution.py:263
  502.8 23.7 %collective-permute-start.33 = (bf16[1,128,2048]{2,1,0:T(8,128)(2,1)S(1)}, bf16[1,128,2048]{2,1,0:T(8,128)(2,1)S(1)}, u32[]{:S(2)}, u32[]{:S(2)}) collective-permute-start(bf16[1,128,2048]{2,1,0:T(8,128)(2,1)S(1)} %slice.495), channel_id=1, source_target_pairs={{0,2},{2,4},{4,6},{6,0},{1,3},{3,5},{5,7},{7,1},{8,10},{10,12},{12... | collective-permute-start | bytes 1572872 | tf_op jit(solution)/shard_map/ppermute | solution.py:264
  502.9 23.5 %collective-permute-start.34 = (bf16[1,128,2048]{2,1,0:T(8,128)(2,1)S(1)}, bf16[1,128,2048]{2,1,0:T(8,128)(2,1)S(1)}, u32[]{:S(2)}, u32[]{:S(2)}) collective-permute-start(bf16[1,128,2048]{2,1,0:T(8,128)(2,1)S(1)} %slice.496), channel_id=1, source_target_pairs={{0,6},{2,0},{4,2},{6,4},{1,7},{3,1},{5,3},{7,5},{8,14},{10,8},{12,... | collective-permute-start | bytes 1572872 | tf_op jit(solution)/shard_map/ppermute | solution.py:265
  519.1 11.2 %collective-permute-start.44 = (bf16[1,128,2048]{2,1,0:T(8,128)(2,1)S(1)}, bf16[1,128,2048]{2,1,0:T(8,128)(2,1)S(1)}, u32[]{:S(2)}, u32[]{:S(2)}) collective-permute-start(bf16[1,128,2048]{2,1,0:T(8,128)(2,1)S(1)} %slice.503), channel_id=1, source_target_pairs={{0,2},{2,4},{4,6},{6,0},{1,3},{3,5},{5,7},{7,1},{8,10},{10,12},{12... | collective-permute-start | bytes 1572872 | tf_op jit(solution)/shard_map/ppermute | solution.py:264
  519.2 11.0 %collective-permute-start.45 = (bf16[1,128,2048]{2,1,0:T(8,128)(2,1)S(1)}, bf16[1,128,2048]{2,1,0:T(8,128)(2,1)S(1)}, u32[]{:S(2)}, u32[]{:S(2)}) collective-permute-start(bf16[1,128,2048]{2,1,0:T(8,128)(2,1)S(1)} %slice.504), channel_id=1, source_target_pairs={{0,6},{2,0},{4,2},{6,4},{1,7},{3,1},{5,3},{7,5},{8,14},{10,8},{12,... | collective-permute-start | bytes 1572872 | tf_op jit(solution)/shard_map/ppermute | solution.py:265
  (93 other events, 1980.0 us)
